TPU v7x, 32 devices: a whole 2x2x4 slice. The times are simulated.
32 devices in a mesh: mx: 8 (over y, x, core), my: 4 (over z).
Axes of the slice: x: 2, y: 2, z: 4, core: 2. Of those that a mesh axis runs over, the one named last changes fastest.
Arguments:
- density: float32 [128, 64, 128], P('mx', 'my'), may hold values from 0.5 to 2
- momentum: float32 [3, 128, 64, 128], P(None, 'mx', 'my'), may hold values from -1.8 to 1.8
- energy: float32 [128, 64, 128], P('mx', 'my'), may hold values from -6 to 6
- entropy: float32 [128, 64, 128], P('mx', 'my'), may hold values from 0.5 to 16, as said below
- tracers: float32 [9, 128, 64, 128], P(None, 'mx', 'my'), may hold values from -6 to 6
- leaf_flags: int32 [16, 8, 16], P('mx', 'my'), may hold values 0 or 1
Outputs:
- section: float32 [15, 128, 64, 128], P(None, 'mx', 'my')
- gravity_accel: float32 [3, 128, 64, 128], P(None, 'mx', 'my')
Inputs may be any that keep to these rules, and one draw needn't show every extreme that they name: `entropy`: positive.
All inputs are finite; a program needn't handle non-finite values. No bound on the sum of `leaf_flags` on one device may be relied on, other than what follows from the above.
Results may differ from a plain program's by a relative error of at most 0.0003.
Values sent between devices are 32-bit elements; how exact they have to be, the bound alone decides.
A program may use at most 128 MiB of HBM per device.

v0:
```python
import math

import jax
import jax.numpy as jnp
import numpy as np
from jax import lax
from jax.sharding import PartitionSpec as P

SUB = 8
LEVELS = 3


gamma_gas = 5.0 / 3.0
courant = 0.3
gravity = 0.02
highest = lax.Precision.HIGHEST
multi_index = [
    (power_x, power_y, degree_sum - power_x - power_y)
    for degree_sum in range(4)
    for power_x in range(degree_sum, -1, -1)
    for power_y in range(degree_sum - power_x, -1, -1)
]


def with_halo(cells, sides, width):
    for axis, dim in sides:
        count = lax.axis_size(axis)
        ends = count - 1
        head = lax.slice_in_dim(cells, 0, width, axis=dim)
        tail = lax.slice_in_dim(cells, cells.shape[dim] - width, cells.shape[dim], axis=dim)
        cells = jnp.concatenate(
            [
                lax.ppermute(tail, axis, [(i, (i + 1) % count) for i in range(ends)]),
                cells,
                lax.ppermute(head, axis, [((i + 1) % count, i) for i in range(ends)]),
            ],
            axis=dim,
        )
    return cells


def factorial_of(exponent):
    return math.factorial(exponent[0]) * math.factorial(exponent[1]) * math.factorial(exponent[2])


def inverse_derivative(exponent, vectors):
    axes_list = [0] * exponent[0] + [1] * exponent[1] + [2] * exponent[2]
    radius = np.sqrt(np.sum(vectors * vectors, axis=1))
    radius_safe = np.where(radius > 0.0, radius, 1.0)
    degree = len(axes_list)
    if degree == 0:
        result = 1.0 / radius_safe
    elif degree == 1:
        result = -vectors[:, axes_list[0]] / radius_safe**3
    elif degree == 2:
        index_one, index_two = axes_list
        result = (
            3.0 * vectors[:, index_one] * vectors[:, index_two] / radius_safe**5
            - float(index_one == index_two) / radius_safe**3
        )
    else:
        index_one, index_two, index_three = axes_list
        crossed = (
            float(index_one == index_two) * vectors[:, index_three]
            + float(index_one == index_three) * vectors[:, index_two]
            + float(index_two == index_three) * vectors[:, index_one]
        )
        result = (
            -15.0
            * vectors[:, index_one]
            * vectors[:, index_two]
            * vectors[:, index_three]
            / radius_safe**7
            + 3.0 * crossed / radius_safe**5
        )
    return np.where(radius > 0.0, result, 0.0)


def offset_grid(reach_x, reach_y, reach_z):
    return [
        (shift_x, shift_y, shift_z)
        for shift_x in range(-reach_x, reach_x + 1)
        for shift_y in range(-reach_y, reach_y + 1)
        for shift_z in range(-reach_z, reach_z + 1)
    ]


def translation_kernel(spacing, offsets):
    vectors = np.asarray(offsets) * (-1.0 * spacing)
    entries = np.zeros((len(offsets), len(multi_index), len(multi_index)))
    for row_index, target_power in enumerate(multi_index):
        for column_index, source_power in enumerate(multi_index):
            if sum(target_power) + sum(source_power) <= 3:
                joined = (
                    target_power[0] + source_power[0],
                    target_power[1] + source_power[1],
                    target_power[2] + source_power[2],
                )
                entries[:, row_index, column_index] = (
                    -gravity
                    * (-1.0) ** sum(source_power)
                    / factorial_of(source_power)
                    * inverse_derivative(joined, vectors)
                )
    return jnp.asarray(entries, dtype=jnp.float32)


def upward_matrices(spacing):
    entries = np.zeros((2, 2, 2, len(multi_index), len(multi_index)))
    for octant in range(8):
        octant_bits = (octant >> 2 & 1, octant >> 1 & 1, octant & 1)
        displacement = [(octant_bits[dimension] - 0.5) * spacing for dimension in range(3)]
        for row_index, target_power in enumerate(multi_index):
            for column_index, source_power in enumerate(multi_index):
                if all(
                    (source_power[dimension] <= target_power[dimension] for dimension in range(3))
                ):
                    entry_value = 1.0
                    for dimension in range(3):
                        entry_value *= math.comb(
                            target_power[dimension], source_power[dimension]
                        ) * displacement[dimension] ** (
                            target_power[dimension] - source_power[dimension]
                        )
                    entries[
                        octant_bits[0], octant_bits[1], octant_bits[2], row_index, column_index
                    ] = entry_value
    return jnp.asarray(entries, dtype=jnp.float32)


def downward_matrices(spacing):
    entries = np.zeros((2, 2, 2, len(multi_index), len(multi_index)))
    for octant in range(8):
        octant_bits = (octant >> 2 & 1, octant >> 1 & 1, octant & 1)
        displacement = [(octant_bits[dimension] - 0.5) * spacing for dimension in range(3)]
        for row_index, target_power in enumerate(multi_index):
            for column_index, source_power in enumerate(multi_index):
                if all(
                    (source_power[dimension] >= target_power[dimension] for dimension in range(3))
                ):
                    entry_value = 1.0
                    for dimension in range(3):
                        lifted = source_power[dimension] - target_power[dimension]
                        entry_value *= displacement[dimension] ** lifted / math.factorial(lifted)
                    entries[
                        octant_bits[0], octant_bits[1], octant_bits[2], row_index, column_index
                    ] = entry_value
    return jnp.asarray(entries, dtype=jnp.float32)


def moment_table(cells_edge):
    centres = (np.arange(cells_edge) + 0.5) / cells_edge - 0.5
    volume = 1.0 / cells_edge**3
    entries = np.zeros((cells_edge, cells_edge, cells_edge, len(multi_index)))
    for column_index, exponent in enumerate(multi_index):
        entries[:, :, :, column_index] = (
            volume
            * centres[:, None, None] ** exponent[0]
            * centres[None, :, None] ** exponent[1]
            * centres[None, None, :] ** exponent[2]
        )
    return jnp.asarray(entries, dtype=jnp.float32)


def field_table(cells_edge):
    centres = (np.arange(cells_edge) + 0.5) / cells_edge - 0.5
    entries = np.zeros((cells_edge, cells_edge, cells_edge, 3, len(multi_index)))
    for column_index, exponent in enumerate(multi_index):
        for dimension in range(3):
            if exponent[dimension] > 0:
                lowered = list(exponent)
                lowered[dimension] -= 1
                entries[:, :, :, dimension, column_index] = (
                    -exponent[dimension]
                    / factorial_of(exponent)
                    * centres[:, None, None] ** lowered[0]
                    * centres[None, :, None] ** lowered[1]
                    * centres[None, None, :] ** lowered[2]
                )
    return jnp.asarray(entries, dtype=jnp.float32)


def allowed(coords, offset, rule_name):
    touching = (jnp.abs(offset[0]) <= 1) & (jnp.abs(offset[1]) <= 1) & (jnp.abs(offset[2]) <= 1)
    accepted = (coords[0] >= 0) & (coords[1] >= 0) & (coords[2] >= 0)
    if rule_name == "coarsest":
        return accepted & jnp.logical_not(touching)
    for dimension in range(3):
        parent_step = jnp.floor_divide(coords[dimension] + offset[dimension], 2) - jnp.floor_divide(
            coords[dimension], 2
        )
        accepted = accepted & (jnp.abs(parent_step) <= 1)
    if rule_name == "finest":
        nonzero = (offset[0] != 0) | (offset[1] != 0) | (offset[2] != 0)
        return accepted & nonzero
    return accepted & jnp.logical_not(touching)


def coordinates(start_x, start_y, block_shape):
    along_x = start_x + jnp.arange(block_shape[0], dtype=jnp.int32)[:, None, None]
    along_y = start_y + jnp.arange(block_shape[1], dtype=jnp.int32)[None, :, None]
    along_z = jnp.arange(block_shape[2], dtype=jnp.int32)[None, None, :]
    return (along_x, along_y, along_z)


def local_from_far(extended, margins, kernels, coords, block_shape, rule_name):
    moments_count = extended.shape[0]
    full_shape = tuple(block_shape)
    reach_x, reach_y, reach_z = margins
    inner_offsets = [
        (shift_y, shift_z)
        for shift_y in range(-reach_y, reach_y + 1)
        for shift_z in range(-reach_z, reach_z + 1)
    ]
    inner_count = len(inner_offsets)
    grouped_kernels = kernels.reshape(2 * reach_x + 1, inner_count, moments_count, moments_count)
    shifts = jnp.arange(-reach_x, reach_x + 1, dtype=jnp.int32)
    cells_count = full_shape[0] * full_shape[1] * full_shape[2]

    def visit(running, item):
        kernel_group, shift_x = item
        slab = lax.dynamic_slice_in_dim(extended, reach_x + shift_x, full_shape[0], axis=1)
        pieces = []
        for shift_y, shift_z in inner_offsets:
            piece = slab[
                :,
                :,
                reach_y + shift_y : reach_y + shift_y + full_shape[1],
                reach_z + shift_z : reach_z + shift_z + full_shape[2],
            ]
            weight = jnp.broadcast_to(
                allowed(coords, (shift_x, shift_y, shift_z), rule_name), full_shape
            ).astype(jnp.float32)
            pieces.append(piece * weight[None])
        stacked = jnp.stack(pieces, axis=0).reshape(inner_count * moments_count, cells_count)
        flat_kernel = jnp.transpose(kernel_group, (1, 0, 2)).reshape(
            moments_count, inner_count * moments_count
        )
        term = jnp.dot(flat_kernel, stacked, precision=highest, preferred_element_type=jnp.float32)
        return (running + term, None)

    initial = jnp.zeros((moments_count, cells_count), jnp.float32)
    running, _ = lax.scan(visit, initial, (grouped_kernels, shifts))
    return running.reshape((moments_count,) + full_shape)


def upward(child, matrices):
    moments_count, size_x, size_y, size_z = child.shape
    grouped = child.reshape(moments_count, size_x // 2, 2, size_y // 2, 2, size_z // 2, 2)
    return jnp.einsum("uvwga,axuyvzw->gxyz", matrices, grouped, precision=highest)


def downward(parent, matrices):
    moments_count, size_x, size_y, size_z = parent.shape
    spread = jnp.einsum("uvwgb,bxyz->gxuyvzw", matrices, parent, precision=highest)
    return spread.reshape(moments_count, 2 * size_x, 2 * size_y, 2 * size_z)


def regroup(gathered, count_x, count_y, piece_shape):
    moments_count, piece_x, piece_y, piece_z = piece_shape
    blocks = gathered.reshape(moments_count, count_x, count_y, piece_x, piece_y, piece_z)
    blocks = jnp.transpose(blocks, (0, 1, 3, 2, 4, 5))
    return blocks.reshape(moments_count, count_x * piece_x, count_y * piece_y, piece_z)


def gravity_local(density, leaf_flags):
    block_x, block_y, block_z = leaf_flags.shape
    cells_edge = density.shape[0] // block_x
    zero_index = jnp.zeros((), jnp.int32)
    grouped = density.reshape(block_x, cells_edge, block_y, cells_edge, block_z, cells_edge)
    moments = jnp.einsum("xaybzc,abcg->gxyz", grouped, moment_table(cells_edge), precision=highest)
    moments = moments * leaf_flags.astype(jnp.float32)[None]
    moments_count = moments.shape[0]
    start_x = lax.axis_index("mx") * block_x
    start_y = lax.axis_index("my") * block_y
    lift_zero = upward_matrices(1.0)
    near_blocks = with_halo(moments, (("mx", 1), ("my", 2)), 2)
    near_ext = jnp.pad(near_blocks, ((0, 0), (1, 1), (1, 1), (3, 3)))
    first_level = upward(moments, lift_zero)
    gathered = lax.all_gather(first_level, ("mx", "my"), axis=1, tiled=True)
    level_one = regroup(gathered, lax.axis_size("mx"), lax.axis_size("my"), first_level.shape)
    levels_list = [level_one]
    for level_index in range(2, LEVELS + 1):
        levels_list.append(upward(levels_list[-1], upward_matrices(2.0 ** (level_index - 1))))
    coarsest = levels_list[-1]
    coarse_shape = coarsest.shape[1:]
    reach_top = (coarse_shape[0] - 1, coarse_shape[1] - 1, coarse_shape[2] - 1)
    top_offsets = offset_grid(reach_top[0], reach_top[1], reach_top[2])
    padded = jnp.pad(
        coarsest,
        (
            (0, 0),
            (reach_top[0], reach_top[0]),
            (reach_top[1], reach_top[1]),
            (reach_top[2], reach_top[2]),
        ),
    )
    expansion = local_from_far(
        padded,
        reach_top,
        translation_kernel(2.0**LEVELS, top_offsets),
        coordinates(0, 0, coarse_shape),
        coarse_shape,
        "coarsest",
    )
    near_offsets = offset_grid(3, 3, 3)
    for level_index in range(LEVELS - 1, 1, -1):
        current = levels_list[level_index - 1]
        block_shape = current.shape[1:]
        padded = jnp.pad(current, ((0, 0), (3, 3), (3, 3), (3, 3)))
        carried = downward(expansion, downward_matrices(2.0**level_index))
        expansion = carried + local_from_far(
            padded,
            (3, 3, 3),
            translation_kernel(2.0**level_index, near_offsets),
            coordinates(0, 0, block_shape),
            block_shape,
            "middle",
        )
    from_parents = downward(expansion, downward_matrices(2.0))
    half_x = block_x // 2
    half_y = block_y // 2
    half_z = block_z // 2
    start_one_x = lax.axis_index("mx") * half_x
    start_one_y = lax.axis_index("my") * half_y
    shape_one = (half_x, half_y, half_z)
    own_parent = lax.dynamic_slice(
        from_parents,
        (zero_index, start_one_x, start_one_y, zero_index),
        (moments_count, half_x, half_y, half_z),
    )
    padded_one = jnp.pad(level_one, ((0, 0), (3, 3), (3, 3), (3, 3)))
    ext_one = lax.dynamic_slice(
        padded_one,
        (zero_index, start_one_x, start_one_y, zero_index),
        (moments_count, half_x + 6, half_y + 6, half_z + 6),
    )
    own_one = own_parent + local_from_far(
        ext_one,
        (3, 3, 3),
        translation_kernel(2.0, near_offsets),
        coordinates(start_one_x, start_one_y, shape_one),
        shape_one,
        "middle",
    )
    shape_zero = (block_x, block_y, block_z)
    own_zero = downward(own_one, downward_matrices(1.0)) + local_from_far(
        near_ext,
        (3, 3, 3),
        translation_kernel(1.0, near_offsets),
        coordinates(start_x, start_y, shape_zero),
        shape_zero,
        "finest",
    )
    accel_cells = jnp.einsum(
        "abcig,gxyz->ixaybzc", field_table(cells_edge), own_zero, precision=highest
    )
    return accel_cells.reshape(3, density.shape[0], density.shape[1], density.shape[2])


def flux_of(states, direction):
    mass_density = states[0]
    velocity = states[1 + direction] / mass_density
    pressure = (gamma_gas - 1.0) * states[5] ** gamma_gas
    sound_speed = jnp.sqrt(gamma_gas * pressure / mass_density)
    flux_vector = states * velocity[None]
    flux_vector = flux_vector.at[1 + direction].add(pressure)
    flux_vector = flux_vector.at[4].add(pressure * velocity)
    return (flux_vector, jnp.abs(velocity) + sound_speed)


def face_flux(extended, direction):
    axis_dim = direction + 1
    faces = extended.shape[axis_dim] - 5
    outer_left, inner_left, left_cell, right_cell, inner_right, outer_right = [
        lax.slice_in_dim(extended, begin_index, begin_index + faces, axis=axis_dim)
        for begin_index in range(6)
    ]
    interface = (
        37.0 * (left_cell + right_cell)
        - 8.0 * (inner_left + inner_right)
        + (outer_left + outer_right)
    ) / 60.0
    left_state = jnp.clip(
        interface,
        jnp.minimum(jnp.minimum(inner_left, left_cell), right_cell),
        jnp.maximum(jnp.maximum(inner_left, left_cell), right_cell),
    )
    right_state = jnp.clip(
        interface,
        jnp.minimum(jnp.minimum(left_cell, right_cell), inner_right),
        jnp.maximum(jnp.maximum(left_cell, right_cell), inner_right),
    )
    flux_left, speed_left = flux_of(left_state, direction)
    flux_right, speed_right = flux_of(right_state, direction)
    speed_face = jnp.maximum(speed_left, speed_right)
    return 0.5 * (flux_left + flux_right) - 0.5 * speed_face[None] * (right_state - left_state)


def cell_speed(conserved):
    velocity = conserved[1:4] / conserved[0][None]
    pressure = (gamma_gas - 1.0) * conserved[5] ** gamma_gas
    sound_speed = jnp.sqrt(gamma_gas * pressure / conserved[0])
    return jnp.max(jnp.abs(velocity), axis=0) + sound_speed


def outer_edges(extended, position, devices_count, axis_dim):
    length = extended.shape[axis_dim]
    edge_low = lax.slice_in_dim(extended, 3, 4, axis=axis_dim)
    edge_high = lax.slice_in_dim(extended, length - 4, length - 3, axis=axis_dim)
    lower_rim = jnp.where(
        position == 0,
        jnp.repeat(edge_low, 3, axis=axis_dim),
        lax.slice_in_dim(extended, 0, 3, axis=axis_dim),
    )
    upper_rim = jnp.where(
        position == devices_count - 1,
        jnp.repeat(edge_high, 3, axis=axis_dim),
        lax.slice_in_dim(extended, length - 3, length, axis=axis_dim),
    )
    middle_part = lax.slice_in_dim(extended, 3, length - 3, axis=axis_dim)
    return jnp.concatenate([lower_rim, middle_part, upper_rim], axis=axis_dim)


def shards(density, momentum, energy, entropy, tracers, leaf_flags):
    conserved = jnp.concatenate(
        [density[None], momentum, energy[None], entropy[None], tracers], axis=0
    )
    extended = with_halo(conserved, (("mx", 1), ("my", 2)), 3)
    extended = outer_edges(extended, lax.axis_index("mx"), lax.axis_size("mx"), 1)
    extended = outer_edges(extended, lax.axis_index("my"), lax.axis_size("my"), 2)
    fastest = lax.pmax(jnp.max(cell_speed(conserved)), ("mx", "my"))
    step_size = courant / (SUB * fastest)
    gravity_accel = gravity_local(density, leaf_flags)
    tendency = jnp.zeros_like(conserved)
    along_x = extended[:, :, 3:-3, :]
    tendency = tendency - jnp.diff(face_flux(along_x, 0), axis=1) * SUB
    along_y = extended[:, 3:-3, :, :]
    tendency = tendency - jnp.diff(face_flux(along_y, 1), axis=2) * SUB
    along_z = jnp.pad(conserved, ((0, 0), (0, 0), (0, 0), (3, 3)), mode="edge")
    tendency = tendency - jnp.diff(face_flux(along_z, 2), axis=3) * SUB
    tendency = tendency.at[1:4].add(density[None] * gravity_accel)
    tendency = tendency.at[4].add(jnp.sum(momentum * gravity_accel, axis=0))
    return (conserved + step_size * tendency, gravity_accel)


def solution(mesh):
    placed = (
        P("mx", "my", None),
        P(None, "mx", "my", None),
        P("mx", "my", None),
        P("mx", "my", None),
        P(None, "mx", "my", None),
        P("mx", "my", None),
    )
    return jax.shard_map(
        shards,
        mesh=mesh,
        in_specs=placed,
        out_specs=(P(None, "mx", "my", None), P(None, "mx", "my", None)),
        check_vma=False,
    )
```

profile of v0, /device:TPU:0, one launch (start us, length us, event | category | flops | bytes accessed | tf_op | source)
XLA Modules:
  0.0 1108.8 jit_solution(16717011865138092742)
XLA Ops:
  0.7 3.4 reshape.6469
  4.9 5.5 fusion.358
  11.7 3.6 collective-permute-start.4
  19.5 5.5 collective-permute-start
  25.0 2.6 fusion.403
  28.1 3.0 copy.5990
  31.1 3.0 copy.5991
  35.3 10.6 maximum_minimum_fusion.1
  45.9 3.2 maximum_minimum_fusion
  50.0 2.9 broadcast_multiply_fusion
  56.2 68.8 %all-gather = f32[20,256]{0,1:T(8,128)S(1)} all-gather(f32[20,8]{0,1:T(8,128)S(1)} %convolution_bitcast_fusion.5), channel_id=2, replica_groups=mesh['mx'=8,'my'=4] {'mx','my'}, dimensions={1}, use_global_device_ids=true | all-gather | bytes 21120 | tf_op jit(solution)/shard_map/all_gather | solution.py:280
  125.1 64.2 %while.76 = (s32[]{:T(128)}, f32[20,8]{0,1:T(8,128)S(1)}, f32[7,49,20,20]{1,3,2,0:T(8,128)}, s32[7]{0:T(128)}, f32[20,7,7,14]{0,3,2,1:T(8,128)S(1)}, /*index=5*/...) while((s32[]{:T(128)}, f32[20,8]{0,1:T(8,128)S(1)}, ...), condition=%wide.region_8.9_spmd.clone.clone, body=%wide.region_7.8_spmd.clone.clone.sunk | while | flops 1898259 | bytes 1128432 | solution.py:243
  190.8 11.7 %while.74 = (s32[]{:T(128)}, f32[20,4]{0,1:T(4,128)S(1)}, f32[3,3,20,20]{3,1,2,0:T(4,128)}, s32[3]{0:T(128)S(1)}, f32[20,4,1,4]{0,3,2,1:T(4,128)S(1)}, /*index=5...) while((s32[]{:T(128)}, f32[20,4]{0,1:T(4,128)S(1)}, ...), condition=%wide.region_4.5_spmd.clone, body=%wide.region_3.4_spmd.clone.sunk | while | flops 58493 | bytes 33533 | solution.py:243
  203.8 482.1 %while.75 = (s32[]{:T(128)}, f32[20,32]{1,0:T(8,128)}, f32[7,49,20,20]{1,3,2,0:T(8,128)}, s32[7]{0:T(128)}, f32[20,10,8,10]{0,3,1,2:T(8,128)S(1)}, /*index=5*/s3...) while((s32[]{:T(128)}, f32[20,32]{1,0:T(8,128)}, ...), condition=%wide.region_6.7_spmd.clone.clone, body=%wide.region_5.6_spmd.clone.clone.sunk | while | flops 7563328 | bytes 5873054 | solution.py:243
  265.2 6.5 reshape.6724
  334.0 6.5 reshape.6724
  402.9 6.5 reshape.6724
  471.7 6.5 reshape.6724
  540.6 6.5 reshape.6724
  609.4 6.5 reshape.6724
  678.2 6.5 reshape.6724
  686.7 2.8 multiply_bitcast_fusion
  689.6 9.8 multiply_subtract_fusion
  703.0 4.6 collective-permute-start.6
  708.2 39.9 %pmax.7 = f32[]{:T(128)} all-reduce(f32[]{:T(128)} %fusion.385), channel_id=1, replica_groups=mesh['mx'=8,'my'=4] {'mx','my'}, use_global_device_ids=true, to_apply=%region_2.3 | all-reduce | flops 1 | bytes 8 | tf_op jit(solution)/shard_map/pmax | solution.py:432
  753.9 5.4 collective-permute-start.2
  759.3 305.1 %while.77 = (s32[]{:T(128)}, f32[20,64]{1,0:T(8,128)}, f32[7,49,20,20]{1,3,2,0:T(8,128)}, s32[7]{0:T(128)}, f32[20,8,8,22]{0,3,2,1:T(8,128)S(1)}, /*index=5*/s32...) while((s32[]{:T(128)}, f32[20,64]{1,0:T(8,128)}, ...), condition=%wide.region_10.11_spmd.clone.clone.clone.clone, body=%wide.region_9.10_spmd.clone.clone.clone.clone.sunk | while | flops 15127043 | bytes 3737995 | solution.py:243
  1065.2 5.5 convolution_bitcast_fusion
  1070.8 5.9 copy.5964
  1076.7 5.3 reshape.6483
  1091.0 4.1 maximum_minimum_fusion.3
  1096.9 3.0 maximum_minimum_fusion.5
  (2819 shorter events, 805.5 us)
Async XLA Ops:
  10.4 690.5 %collective-permute-start.5 = (f32[20,2,2,16]{0,3,2,1:T(8,128)}, f32[20,2,2,16]{0,3,2,1:T(8,128)}, u32[]{:S(2)}, u32[]{:S(2)}) collective-permute-start(f32[20,2,2,16]{0,3,2,1:T(8,128)} %fusion.358), channel_id=1, source_target_pairs={{4,0},{8,4},{12,8},{16,12},{20,16},{24,20},{28,24},{5,1},{9,5},{13... | collective-permute-start | bytes 15368 | tf_op jit(solution)/shard_map/ppermute | solution.py:35
  11.7 689.2 %collective-permute-start.4 = (f32[20,2,2,16]{0,3,2,1:T(8,128)}, f32[20,2,2,16]{0,3,2,1:T(8,128)}, u32[]{:S(2)}, u32[]{:S(2)}) collective-permute-start(f32[20,2,2,16]{0,3,2,1:T(8,128)} %fusion.358), channel_id=1, source_target_pairs={{0,4},{4,8},{8,12},{12,16},{16,20},{20,24},{24,28},{1,5},{5,9},{9,... | collective-permute-start | bytes 15368 | tf_op jit(solution)/shard_map/ppermute | solution.py:33
  16.8 733.6 %copy-start = (f32[15,16,16,128]{3,1,2,0:T(8,128)}, f32[15,16,16,128]{3,1,2,0:T(8,128)S(1)}, u32[]{:S(2)}) copy-start(f32[15,16,16,128]{3,1,2,0:T(8,128)S(1)} %copy_dynamic-update-slice_fusion) | copy-start | bytes 5898244
  18.2 732.2 %collective-permute-start.1 = (f32[15,3,16,128]{3,1,2,0:T(4,128)}, f32[15,3,16,128]{3,1,2,0:T(4,128)}, u32[]{:S(2)}, u32[]{:S(2)}) collective-permute-start(f32[15,3,16,128]{3,1,2,0:T(4,128)} %get-tuple-element.3868), channel_id=1, source_target_pairs={{4,0},{8,4},{12,8},{16,12},{20,16},{24,20},{28,24},{5,1},{9,5},{13... | collective-permute-start | bytes 1105928 | tf_op jit(solution)/shard_map/ppermute | solution.py:35
  19.5 730.9 %collective-permute-start = (f32[15,3,16,128]{3,1,2,0:T(4,128)}, f32[15,3,16,128]{3,1,2,0:T(4,128)}, u32[]{:S(2)}, u32[]{:S(2)}) collective-permute-start(f32[15,3,16,128]{3,1,2,0:T(4,128)} %get-tuple-element.3867), channel_id=1, source_target_pairs={{0,4},{4,8},{8,12},{12,16},{16,20},{20,24},{24,28},{1,5},{5,9},{9,... | collective-permute-start | bytes 1105928 | tf_op jit(solution)/shard_map/ppermute | solution.py:33
  125.0 65.6 %copy-start.59 = (f32[2,2,2,20,20,1]{4,3,2,5,1,0:T(8,128)S(1)}, f32[2,2,2,20,20,1]{4,3,2,5,1,0:T(8,128)}, u32[]{:S(2)}) copy-start(f32[2,2,2,20,20,1]{4,3,2,5,1,0:T(8,128)} %constant.2966) | copy-start | bytes 38404
  125.1 77.5 %copy-start.58 = (f32[2,2,2,20,20,1]{4,3,2,1,0,5:T(8,128)S(1)}, f32[2,2,2,20,20,1]{4,3,2,1,0,5:T(8,128)}, u32[]{:S(2)}) copy-start(f32[2,2,2,20,20,1]{4,3,2,1,0,5:T(8,128)} %constant.2969) | copy-start | bytes 38404
  218.3 24.1 %copy-start.46 = (f32[4,2,4]{2,1,0:T(2,128)S(1)}, f32[4,2,4]{2,1,0:T(2,128)}, u32[]{:S(2)}) copy-start(f32[4,2,4]{2,1,0:T(2,128)} %get-tuple-element.4334) | copy-start | bytes 388 | tf_op jit(solution)/shard_map/while
  220.0 24.1 %copy-start.45 = (f32[4,2,4]{2,1,0:T(2,128)S(1)}, f32[4,2,4]{2,1,0:T(2,128)}, u32[]{:S(2)}) copy-start(f32[4,2,4]{2,1,0:T(2,128)} %get-tuple-element.4338) | copy-start | bytes 388 | tf_op jit(solution)/shard_map/while
  221.5 23.4 %copy-start.44 = (f32[4,2,4]{2,1,0:T(2,128)S(1)}, f32[4,2,4]{2,1,0:T(2,128)}, u32[]{:S(2)}) copy-start(f32[4,2,4]{2,1,0:T(2,128)} %get-tuple-element.4340) | copy-start | bytes 388 | tf_op jit(solution)/shard_map/while
  287.1 24.1 %copy-start.46 = (f32[4,2,4]{2,1,0:T(2,128)S(1)}, f32[4,2,4]{2,1,0:T(2,128)}, u32[]{:S(2)}) copy-start(f32[4,2,4]{2,1,0:T(2,128)} %get-tuple-element.4334) | copy-start | bytes 388 | tf_op jit(solution)/shard_map/while
  288.8 24.1 %copy-start.45 = (f32[4,2,4]{2,1,0:T(2,128)S(1)}, f32[4,2,4]{2,1,0:T(2,128)}, u32[]{:S(2)}) copy-start(f32[4,2,4]{2,1,0:T(2,128)} %get-tuple-element.4338) | copy-start | bytes 388 | tf_op jit(solution)/shard_map/while
  290.4 23.4 %copy-start.44 = (f32[4,2,4]{2,1,0:T(2,128)S(1)}, f32[4,2,4]{2,1,0:T(2,128)}, u32[]{:S(2)}) copy-start(f32[4,2,4]{2,1,0:T(2,128)} %get-tuple-element.4340) | copy-start | bytes 388 | tf_op jit(solution)/shard_map/while
  355.9 24.1 %copy-start.46 = (f32[4,2,4]{2,1,0:T(2,128)S(1)}, f32[4,2,4]{2,1,0:T(2,128)}, u32[]{:S(2)}) copy-start(f32[4,2,4]{2,1,0:T(2,128)} %get-tuple-element.4334) | copy-start | bytes 388 | tf_op jit(solution)/shard_map/while
  357.7 24.1 %copy-start.45 = (f32[4,2,4]{2,1,0:T(2,128)S(1)}, f32[4,2,4]{2,1,0:T(2,128)}, u32[]{:S(2)}) copy-start(f32[4,2,4]{2,1,0:T(2,128)} %get-tuple-element.4338) | copy-start | bytes 388 | tf_op jit(solution)/shard_map/while
  359.2 23.4 %copy-start.44 = (f32[4,2,4]{2,1,0:T(2,128)S(1)}, f32[4,2,4]{2,1,0:T(2,128)}, u32[]{:S(2)}) copy-start(f32[4,2,4]{2,1,0:T(2,128)} %get-tuple-element.4340) | copy-start | bytes 388 | tf_op jit(solution)/shard_map/while
  424.8 24.1 %copy-start.46 = (f32[4,2,4]{2,1,0:T(2,128)S(1)}, f32[4,2,4]{2,1,0:T(2,128)}, u32[]{:S(2)}) copy-start(f32[4,2,4]{2,1,0:T(2,128)} %get-tuple-element.4334) | copy-start | bytes 388 | tf_op jit(solution)/shard_map/while
  426.5 24.1 %copy-start.45 = (f32[4,2,4]{2,1,0:T(2,128)S(1)}, f32[4,2,4]{2,1,0:T(2,128)}, u32[]{:S(2)}) copy-start(f32[4,2,4]{2,1,0:T(2,128)} %get-tuple-element.4338) | copy-start | bytes 388 | tf_op jit(solution)/shard_map/while
  428.1 23.4 %copy-start.44 = (f32[4,2,4]{2,1,0:T(2,128)S(1)}, f32[4,2,4]{2,1,0:T(2,128)}, u32[]{:S(2)}) copy-start(f32[4,2,4]{2,1,0:T(2,128)} %get-tuple-element.4340) | copy-start | bytes 388 | tf_op jit(solution)/shard_map/while
  493.6 24.1 %copy-start.46 = (f32[4,2,4]{2,1,0:T(2,128)S(1)}, f32[4,2,4]{2,1,0:T(2,128)}, u32[]{:S(2)}) copy-start(f32[4,2,4]{2,1,0:T(2,128)} %get-tuple-element.4334) | copy-start | bytes 388 | tf_op jit(solution)/shard_map/while
  495.4 24.1 %copy-start.45 = (f32[4,2,4]{2,1,0:T(2,128)S(1)}, f32[4,2,4]{2,1,0:T(2,128)}, u32[]{:S(2)}) copy-start(f32[4,2,4]{2,1,0:T(2,128)} %get-tuple-element.4338) | copy-start | bytes 388 | tf_op jit(solution)/shard_map/while
  562.5 24.1 %copy-start.46 = (f32[4,2,4]{2,1,0:T(2,128)S(1)}, f32[4,2,4]{2,1,0:T(2,128)}, u32[]{:S(2)}) copy-start(f32[4,2,4]{2,1,0:T(2,128)} %get-tuple-element.4334) | copy-start | bytes 388 | tf_op jit(solution)/shard_map/while
  564.2 24.1 %copy-start.45 = (f32[4,2,4]{2,1,0:T(2,128)S(1)}, f32[4,2,4]{2,1,0:T(2,128)}, u32[]{:S(2)}) copy-start(f32[4,2,4]{2,1,0:T(2,128)} %get-tuple-element.4338) | copy-start | bytes 388 | tf_op jit(solution)/shard_map/while
  565.7 23.4 %copy-start.44 = (f32[4,2,4]{2,1,0:T(2,128)S(1)}, f32[4,2,4]{2,1,0:T(2,128)}, u32[]{:S(2)}) copy-start(f32[4,2,4]{2,1,0:T(2,128)} %get-tuple-element.4340) | copy-start | bytes 388 | tf_op jit(solution)/shard_map/while
  631.3 24.1 %copy-start.46 = (f32[4,2,4]{2,1,0:T(2,128)S(1)}, f32[4,2,4]{2,1,0:T(2,128)}, u32[]{:S(2)}) copy-start(f32[4,2,4]{2,1,0:T(2,128)} %get-tuple-element.4334) | copy-start | bytes 388 | tf_op jit(solution)/shard_map/while
  633.0 24.1 %copy-start.45 = (f32[4,2,4]{2,1,0:T(2,128)S(1)}, f32[4,2,4]{2,1,0:T(2,128)}, u32[]{:S(2)}) copy-start(f32[4,2,4]{2,1,0:T(2,128)} %get-tuple-element.4338) | copy-start | bytes 388 | tf_op jit(solution)/shard_map/while
  634.6 23.4 %copy-start.44 = (f32[4,2,4]{2,1,0:T(2,128)S(1)}, f32[4,2,4]{2,1,0:T(2,128)}, u32[]{:S(2)}) copy-start(f32[4,2,4]{2,1,0:T(2,128)} %get-tuple-element.4340) | copy-start | bytes 388 | tf_op jit(solution)/shard_map/while
  701.7 47.7 %collective-permute-start.7 = (f32[20,6,2,16]{0,3,2,1:T(8,128)S(1)}, f32[20,6,2,16]{0,3,2,1:T(8,128)S(1)}, u32[]{:S(2)}, u32[]{:S(2)}) collective-permute-start(f32[20,6,2,16]{0,3,2,1:T(8,128)S(1)} %pad_maximum_fusion.14), channel_id=1, source_target_pairs={{1,0},{2,1},{3,2},{5,4},{6,5},{7,6},{9,8},{10,9},{11,10},{13,12},{... | collective-permute-start | bytes 46088 | tf_op jit(solution)/shard_map/ppermute | solution.py:35
  703.0 46.5 %collective-permute-start.6 = (f32[20,6,2,16]{0,3,2,1:T(8,128)S(1)}, f32[20,6,2,16]{0,3,2,1:T(8,128)S(1)}, u32[]{:S(2)}, u32[]{:S(2)}) collective-permute-start(f32[20,6,2,16]{0,3,2,1:T(8,128)S(1)} %pad_maximum_fusion.14), channel_id=1, source_target_pairs={{0,1},{1,2},{2,3},{4,5},{5,6},{6,7},{8,9},{9,10},{10,11},{12,13},{... | collective-permute-start | bytes 46088 | tf_op jit(solution)/shard_map/ppermute | solution.py:33
  751.7 330.3 %collective-permute-start.3 = (f32[15,22,3,128]{3,0,2,1:T(8,128)S(1)}, f32[15,22,3,128]{3,0,2,1:T(8,128)}, u32[]{:S(2)}, u32[]{:S(2)}) collective-permute-start(f32[15,22,3,128]{3,0,2,1:T(8,128)S(1)} %copy.5927), channel_id=1, source_target_pairs={{1,0},{2,1},{3,2},{5,4},{6,5},{7,6},{9,8},{10,9},{11,10},{13,12},{... | collective-permute-start | bytes 1520648 | tf_op jit(solution)/shard_map/ppermute | solution.py:35
  753.9 329.5 %collective-permute-start.2 = (f32[15,22,3,128]{3,0,2,1:T(8,128)}, f32[15,22,3,128]{3,0,2,1:T(8,128)}, u32[]{:S(2)}, u32[]{:S(2)}) collective-permute-start(f32[15,22,3,128]{3,0,2,1:T(8,128)} %copy.5926), channel_id=1, source_target_pairs={{0,1},{1,2},{2,3},{4,5},{5,6},{6,7},{8,9},{9,10},{10,11},{12,13},{... | collective-permute-start | bytes 1520648 | tf_op jit(solution)/shard_map/ppermute | solution.py:33
  1081.9 24.2 %copy-start.7 = (f32[3,16,16,128]{3,2,1,0:T(8,128)}, f32[3,16,16,128]{3,2,1,0:T(8,128)S(1)}, u32[]{:S(2)}) copy-start(f32[3,16,16,128]{3,2,1,0:T(8,128)S(1)} %reshape.6483) | copy-start | bytes 1179652
  (263 other events, 4313.2 us)
where the time goes:
time: 1120 us; the launch traced here: 1110 us
  local copies, waits for them, and re-layouts  457 us (41%)
  other arithmetic  437 us (39%)
  blocking collectives  109 us (10%)
  loops' own time  57.2 us (5%)
  starting transfers between devices  24.2 us (2%)
  matrix products  22.2 us (2%)
    while x672, other arithmetic  252 us
    while x854, local copies, waits for them, and re-layouts  224 us
    mul x147, other arithmetic, visit(): pieces.append(piece * weight[None])  82.6 us
    all_gather x1, blocking collectives, gravity_local(): gathered = lax.all_gather(first_level, ('mx', 'my'), axis=1, tiled=True)  68.8 us
    another operation x4, loops' own time, local_from_far(): running, _ = lax.scan(visit, initial, (grouped_kernels, shifts))  57.2 us
    another operation x220, local copies, waits for them, and re-layouts, visit(): jnp.stack(pieces, axis=0).reshape(inner_count * moments_count, cells_count)  52 us
    reshape x24, local copies, waits for them, and re-layouts, visit(): jnp.stack(pieces, axis=0).reshape(inner_count * moments_count, cells_count)  49.5 us
    pmax x1, blocking collectives, shards(): fastest = lax.pmax(jnp.max(cell_speed(conserved)), ('mx', 'my'))  39.9 us
  transfers between devices with their start and end apart: 8, of which 0 were waited for; matrix products, arithmetic and copies ran while one was open for 78% of the time, Pallas kernels for 0%

commit v1 on v0

v1 whole, which is shorter than its diff:
```python
import functools
import math

import jax
import jax.numpy as jnp
import numpy as np
from jax import lax
from jax.experimental import pallas as pl
from jax.experimental.pallas import tpu as pltpu
from jax.sharding import PartitionSpec as P

MESH = pl.DeviceIdType.MESH
SUB = 8
LEVELS = 3


gamma_gas = 5.0 / 3.0
courant = 0.3
gravity = 0.02
highest = lax.Precision.HIGHEST
multi_index = [
    (power_x, power_y, degree_sum - power_x - power_y)
    for degree_sum in range(4)
    for power_x in range(degree_sum, -1, -1)
    for power_y in range(degree_sum - power_x, -1, -1)
]


def factorial_of(exponent):
    return math.factorial(exponent[0]) * math.factorial(exponent[1]) * math.factorial(exponent[2])


def inverse_derivative(exponent, vectors):
    axes_list = [0] * exponent[0] + [1] * exponent[1] + [2] * exponent[2]
    radius = np.sqrt(np.sum(vectors * vectors, axis=1))
    radius_safe = np.where(radius > 0.0, radius, 1.0)
    degree = len(axes_list)
    if degree == 0:
        result = 1.0 / radius_safe
    elif degree == 1:
        result = -vectors[:, axes_list[0]] / radius_safe**3
    elif degree == 2:
        index_one, index_two = axes_list
        result = (
            3.0 * vectors[:, index_one] * vectors[:, index_two] / radius_safe**5
            - float(index_one == index_two) / radius_safe**3
        )
    else:
        index_one, index_two, index_three = axes_list
        crossed = (
            float(index_one == index_two) * vectors[:, index_three]
            + float(index_one == index_three) * vectors[:, index_two]
            + float(index_two == index_three) * vectors[:, index_one]
        )
        result = (
            -15.0
            * vectors[:, index_one]
            * vectors[:, index_two]
            * vectors[:, index_three]
            / radius_safe**7
            + 3.0 * crossed / radius_safe**5
        )
    return np.where(radius > 0.0, result, 0.0)


def offset_grid(reach_x, reach_y, reach_z):
    return [
        (shift_x, shift_y, shift_z)
        for shift_x in range(-reach_x, reach_x + 1)
        for shift_y in range(-reach_y, reach_y + 1)
        for shift_z in range(-reach_z, reach_z + 1)
    ]


def translation_kernel(spacing, offsets):
    vectors = np.asarray(offsets) * (-1.0 * spacing)
    entries = np.zeros((len(offsets), len(multi_index), len(multi_index)))
    for row_index, target_power in enumerate(multi_index):
        for column_index, source_power in enumerate(multi_index):
            if sum(target_power) + sum(source_power) <= 3:
                joined = (
                    target_power[0] + source_power[0],
                    target_power[1] + source_power[1],
                    target_power[2] + source_power[2],
                )
                entries[:, row_index, column_index] = (
                    -gravity
                    * (-1.0) ** sum(source_power)
                    / factorial_of(source_power)
                    * inverse_derivative(joined, vectors)
                )
    return entries.astype(np.float32)


def upward_matrices(spacing):
    entries = np.zeros((2, 2, 2, len(multi_index), len(multi_index)))
    for octant in range(8):
        octant_bits = (octant >> 2 & 1, octant >> 1 & 1, octant & 1)
        displacement = [(octant_bits[dimension] - 0.5) * spacing for dimension in range(3)]
        for row_index, target_power in enumerate(multi_index):
            for column_index, source_power in enumerate(multi_index):
                if all(
                    (source_power[dimension] <= target_power[dimension] for dimension in range(3))
                ):
                    entry_value = 1.0
                    for dimension in range(3):
                        entry_value *= math.comb(
                            target_power[dimension], source_power[dimension]
                        ) * displacement[dimension] ** (
                            target_power[dimension] - source_power[dimension]
                        )
                    entries[
                        octant_bits[0], octant_bits[1], octant_bits[2], row_index, column_index
                    ] = entry_value
    return entries.astype(np.float32)


def downward_matrices(spacing):
    entries = np.zeros((2, 2, 2, len(multi_index), len(multi_index)))
    for octant in range(8):
        octant_bits = (octant >> 2 & 1, octant >> 1 & 1, octant & 1)
        displacement = [(octant_bits[dimension] - 0.5) * spacing for dimension in range(3)]
        for row_index, target_power in enumerate(multi_index):
            for column_index, source_power in enumerate(multi_index):
                if all(
                    (source_power[dimension] >= target_power[dimension] for dimension in range(3))
                ):
                    entry_value = 1.0
                    for dimension in range(3):
                        lifted = source_power[dimension] - target_power[dimension]
                        entry_value *= displacement[dimension] ** lifted / math.factorial(lifted)
                    entries[
                        octant_bits[0], octant_bits[1], octant_bits[2], row_index, column_index
                    ] = entry_value
    return entries.astype(np.float32)


slot = 128
wide = 256
count_m = len(multi_index)
degrees = np.array([sum(exponent) for exponent in multi_index])
inner_columns = [
    (dx * 3 + dy) * 4 + bx * 2 + by
    for dx in range(3)
    for dy in range(3)
    for bx in range(2)
    for by in range(2)
    if 1 <= 2 * dx + bx <= 4 and 1 <= 2 * dy + by <= 4
]


def split_pair(table):
    table = jnp.asarray(table, jnp.float32)
    high = table.astype(jnp.bfloat16)
    return high, (table - high.astype(jnp.float32)).astype(jnp.bfloat16)


def window_tables():
    columns = [
        (2 * dx - 2 + bx, 2 * dy - 2 + by)
        for dx in range(3)
        for dy in range(3)
        for bx in range(2)
        for by in range(2)
    ]
    children = [(i >> 2 & 1, i >> 1 & 1, i & 1) for i in range(8)]
    sources = [(cx, cy, sz - 2) for cx, cy in columns for sz in range(6)]
    offsets = np.array([[[s[k] - t[k] for k in range(3)] for t in children] for s in sources])
    kernels = np.asarray(translation_kernel(1.0, offsets.reshape(-1, 3)), np.float64)
    kernels = kernels.reshape(36, 6, 8, count_m, count_m)
    touching = (np.abs(offsets).max(axis=2) <= 1).reshape(36, 6, 8, 1, 1)

    def laid(part):
        out = np.zeros((36, slot, 8, 32))
        out[:, : 6 * count_m, :, :count_m] = part.transpose(0, 1, 4, 2, 3).reshape(
            36, 6 * count_m, 8, count_m
        )
        return out.reshape(36, slot, wide)

    middle = laid(np.where(touching, 0.0, kernels))
    close = laid(np.where(touching, kernels, 0.0))[np.array(inner_columns)]
    return middle.reshape(-1, wide), close.reshape(-1, wide)


def moment_tables(cells_z):
    centres = (np.arange(SUB) + 0.5) / SUB - 0.5
    spread = np.zeros((2, 4, 2, SUB, 4, slot))
    along_z = np.zeros((cells_z, 4, slot))
    pick_up = np.zeros((4, slot, slot))
    lift = np.asarray(upward_matrices(1.0), np.float64)
    lift_two = np.asarray(upward_matrices(2.0), np.float64)
    second = np.zeros((4, slot, 2 * slot))
    for sd in range(6):
        for index, power in enumerate(multi_index):
            lane = sd * count_m + index
            for bx in range(2):
                for by in range(2):
                    spread[bx, power[0], by, :, bx * 2 + by, lane] = (
                        centres ** power[1] / SUB**3
                    )
            along_z[:, :, lane] = (np.tile(centres, cells_z // SUB) ** power[2])[:, None]
            for bx in range(2):
                for by in range(2):
                    for dz in range(2):
                        for lower in range(count_m):
                            pick_up[bx * 2 + by, (2 + dz) * count_m + lower, lane] = (
                                lift[bx, by, dz, index, lower] * 0.5 ** sum(power)
                            )
                            second[bx * 2 + by, lower, dz * slot + lane] = (
                                lift_two[bx, by, dz, index, lower]
                                * 2.0 ** degrees[lower]
                                * 0.25 ** sum(power)
                            )
    parents = cells_z // SUB // 2
    rows = np.arange(8)
    cell_rows = np.zeros((6, 8, cells_z))
    one_rows = np.zeros((6, 8, 8))
    two_rows = np.zeros((2, 6, 8, 8))
    for s in range(3):
        for dz in range(2):
            sd = s * 2 + dz
            for row in rows:
                cell_rows[sd, row] = np.arange(cells_z) // SUB == 2 * (row + s - 1) + dz
                if row < parents // 2:
                    one_rows[sd, row] = rows == 2 * (row + s - 1) + dz
                if 4 <= row < 4 + parents // 4:
                    second_z = 2 * (row - 4 + s - 1) + dz
                    if 0 <= second_z < parents // 2:
                        for dz_one in range(2):
                            two_rows[dz_one, sd, row] = rows == 2 * second_z + dz_one
    return (
        spread.reshape(128, 4 * slot),
        along_z.reshape(cells_z, 4 * slot),
        cell_rows.reshape(48, cells_z),
        pick_up.reshape(4 * slot, slot),
        one_rows.reshape(48, 8),
        second,
        two_rows.reshape(96, 8),
        (np.arange(cells_z)[None, :] // SUB == np.arange(cells_z // SUB)[:, None]).astype(float),
    )


def down_tables(cells_z):
    def stacked(spacing):
        down = np.asarray(downward_matrices(spacing), np.float64)
        out = np.zeros((2, 2, 2, 32, 2, 32))
        for bz in range(2):
            for child in range(2):
                out[:, :, bz, :count_m, child, :count_m] = down[:, :, child].transpose(0, 1, 3, 2)
        return out

    scale = np.zeros((16, 8, 32))
    scale[:8, :, :count_m] = 1.0
    scale[8:12, :, :count_m] = 0.5 ** (degrees + 1)
    scale[12:14, :, :count_m] = 0.25 ** (degrees + 1)
    near = stacked(1.0)
    near = near.transpose(2, 3, 0, 1, 4, 5).reshape(64, wide)
    rows = np.arange(8)
    take_one = (np.arange(16)[None, :] == 8 + rows[:, None]) & (rows[:, None] < 4)
    take_two = (np.arange(16)[None, :] == 12 + rows[:, None] // 2) & (rows[:, None] < 4)
    take_zero = np.arange(8)[None, :] == rows[:, None] // 2
    centres = (np.arange(SUB) + 0.5) / SUB - 0.5
    to_z = np.arange(cells_z)[None, :] // (2 * SUB) == rows[:, None]
    heights = np.tile(centres, cells_z // SUB)
    bz_of = np.arange(cells_z) // SUB % 2
    weights = np.zeros((2, 2, 2, 2, 32, cells_z))
    fields = np.zeros((3, 2, 3, 2, SUB, 2, 2, 2, 32))
    for index, power in enumerate(multi_index):
        for bz in range(2):
            weights[0, :, :, bz, index] = (bz_of == bz) * heights ** power[2]
            if power[2] > 0:
                weights[1, :, :, bz, index] = (bz_of == bz) * heights ** (power[2] - 1)
        for k in range(3):
            if power[k] > 0:
                lowered = list(power)
                lowered[k] -= 1
                for bx in range(2):
                    for by in range(2):
                        fields[k, bx, lowered[0], by, :, bx, by, :, index] = (
                            -power[k] / factorial_of(power) * centres ** lowered[1]
                        )[:, None]
    return (
        scale.reshape(16, wide),
        stacked(2.0).reshape(4, 64, 64),
        near,
        take_one.astype(float),
        take_two.astype(float),
        take_zero.astype(float),
        to_z.astype(float),
        weights.reshape(2, wide, cells_z),
        fields.reshape(3, 96, wide),
    )


def top_tables(nx, ny):
    lift = np.asarray(upward_matrices(4.0), np.float64)
    raise_up = np.zeros((4, slot, slot))
    lower_down = np.zeros((4, slot, 64))
    down = np.asarray(downward_matrices(4.0), np.float64)
    for bx in range(2):
        for by in range(2):
            for dz in range(2):
                raise_up[bx * 2 + by, (2 + dz) * count_m : (3 + dz) * count_m, :count_m] = (
                    lift[bx, by, dz] * 4.0 ** degrees[None, :]
                ).T
                lower_down[bx * 2 + by, :count_m, dz * 32 : dz * 32 + count_m] = down[bx, by, dz].T
    offsets = np.array(offset_grid(nx - 1, ny - 1, 1))
    kernels = np.asarray(translation_kernel(8.0, offsets), np.float64)
    counting = np.abs(offsets).max(axis=1) > 1
    far = np.zeros((len(offsets), slot, slot))
    far[:, :count_m, :count_m] = (kernels * counting[:, None, None]).transpose(0, 2, 1)
    return bool(counting.any()), raise_up, lower_down, far


def exact(left, right):
    return jnp.dot(left, right, precision=highest, preferred_element_type=jnp.float32)


def contract_rows(left, right):
    return lax.dot_general(
        left, right, (((0,), (0,)), ((), ())), precision=highest,
        preferred_element_type=jnp.float32,
    )


def sound(entropy, inverse):
    pressure = (gamma_gas - 1.0) * jnp.exp(gamma_gas * jnp.log(entropy))
    return pressure, jnp.sqrt(gamma_gas * pressure * inverse)


def states_of(stencil):
    a, b, c, d, e, f = stencil
    interface = (37.0 / 60.0) * (c + d) - (8.0 / 60.0) * (b + e) + (1.0 / 60.0) * (a + f)
    low, high = jnp.minimum(c, d), jnp.maximum(c, d)
    left = jnp.minimum(jnp.maximum(interface, jnp.minimum(b, low)), jnp.maximum(b, high))
    right = jnp.minimum(jnp.maximum(interface, jnp.minimum(e, low)), jnp.maximum(e, high))
    return left, right


def emit_fluxes(stencil_of, direction, count_fields, emit):
    mass = states_of(stencil_of(0))
    push = states_of(stencil_of(1 + direction))
    heat = states_of(stencil_of(5))
    inverse = [1.0 / value for value in mass]
    speed = [push[i] * inverse[i] for i in range(2)]
    gas = [sound(heat[i], inverse[i]) for i in range(2)]
    fastest = jnp.maximum(jnp.abs(speed[0]) + gas[0][1], jnp.abs(speed[1]) + gas[1][1])
    weight_left = 0.5 * (speed[0] + fastest)
    weight_right = 0.5 * (speed[1] - fastest)
    for field in range(count_fields):
        known = {0: mass, 1 + direction: push, 5: heat}
        left, right = known[field] if field in known else states_of(stencil_of(field))
        flux = left * weight_left + right * weight_right
        if field == 1 + direction:
            flux = flux + 0.5 * (gas[0][0] + gas[1][0])
        if field == 4:
            flux = flux + 0.5 * (gas[0][0] * speed[0] + gas[1][0] * speed[1])
        emit(field, flux)


def section_kernel(
    sizes, top,
    density, momentum, energy, entropy, tracers, flags,
    middle_hi, middle_lo, close_hi, close_lo,
    spread, along_z, cell_rows, pick_up, one_rows, second, two_rows, flag_z,
    scale, down_two, down_one, take_one, take_two, take_zero, to_z, weights, fields,
    raise_up, lower_down, far,
    section, accel,
    ext_x, ext_y, moved, previous, packed, packed_flux, tiles, near, window, rows_p,
    mid_hi, mid_lo, cls_hi, cls_lo,
    load_sem, table_sem, halo_send, halo_recv, first_send, first_recv,
    second_send, second_recv, side_send, side_recv,
):
    count_x, count_y, nf, cx, cy, cz = sizes
    mx, my = lax.axis_index("mx"), lax.axis_index("my")
    loads = [
        pltpu.make_async_copy(source, ext_x.at[pl.ds(begin, size), pl.ds(3, cx)], load_sem.at[i])
        for i, (source, begin, size) in enumerate(
            [(density, 0, 1), (momentum, 1, 3), (energy, 4, 1), (entropy, 5, 1), (tracers, 6, nf - 6)]
        )
    ]
    tables = [
        pltpu.make_async_copy(source, target, table_sem.at[i])
        for i, (source, target) in enumerate(
            [(middle_hi, mid_hi), (middle_lo, mid_lo), (close_hi, cls_hi), (close_lo, cls_lo)]
        )
    ]
    for copy in loads:
        copy.start()
    for copy in tables:
        copy.start()

    def at_x(step):
        return (lax.rem(mx + step + count_x, count_x), my)

    def at_y(step):
        return (mx, lax.rem(my + step + count_y, count_y))

    barrier = pltpu.get_barrier_semaphore()
    for step in range(1, count_x):
        pl.semaphore_signal(barrier, inc=1, device_id=at_x(step), device_id_type=MESH)
    for step in range(1, count_y):
        pl.semaphore_signal(barrier, inc=1, device_id=at_y(step), device_id_type=MESH)
    pl.semaphore_wait(barrier, count_x + count_y - 2)
    for copy in loads:
        copy.wait()

    def remote(source, target, send, recv, device):
        return pltpu.make_async_remote_copy(
            src_ref=source, dst_ref=target, send_sem=send, recv_sem=recv,
            device_id=device, device_id_type=MESH,
        )

    def halo_pair(buffer, length, base, place):
        lower = remote(
            buffer.at[:, pl.ds(3, 3)], buffer.at[:, pl.ds(length + 3, 3)],
            halo_send.at[base], halo_recv.at[base], place(-1),
        )
        upper = remote(
            buffer.at[:, pl.ds(length, 3)], buffer.at[:, pl.ds(0, 3)],
            halo_send.at[base + 1], halo_recv.at[base + 1], place(1),
        )
        return lower, upper

    def start_halo(pair, position, count):
        @pl.when(position > 0)
        def _():
            pair[0].start()

        @pl.when(position < count - 1)
        def _():
            pair[1].start()

    def finish_halo(pair, buffer, length, position, count):
        @pl.when(position > 0)
        def _():
            pair[0].wait_send()
            pair[1].wait_recv()

        @pl.when(position < count - 1)
        def _():
            pair[1].wait_send()
            pair[0].wait_recv()

        @pl.when(position == 0)
        def _():
            for row in range(3):
                buffer[:, row] = buffer[:, 3]

        @pl.when(position == count - 1)
        def _():
            for row in range(3):
                buffer[:, length + 3 + row] = buffer[:, length + 2]

    pair_x = halo_pair(ext_x, cx, 0, at_x)
    pair_y = halo_pair(ext_y, cy, 2, at_y)

    def turn(field, carry):
        for row in range(cy):
            ext_y[field, 3 + row] = ext_x[field, pl.ds(3, cx), row, :]
        return carry

    lax.fori_loop(0, nf, turn, 0)
    start_halo(pair_y, my, count_y)
    start_halo(pair_x, mx, count_x)

    def cell_speed(row, best):
        inverse = 1.0 / ext_x[0, 3 + row]
        largest = jnp.maximum(
            jnp.maximum(jnp.abs(ext_x[1, 3 + row]), jnp.abs(ext_x[2, 3 + row])),
            jnp.abs(ext_x[3, 3 + row]),
        )
        _, speed = sound(ext_x[5, 3 + row], inverse)
        return jnp.maximum(best, largest * inverse + speed)

    best = lax.fori_loop(0, cx, cell_speed, jnp.zeros((cy, cz), jnp.float32))
    best = jnp.max(best)

    for bx in range(2):
        flagged = jnp.concatenate(
            [
                exact(
                    jnp.broadcast_to(
                        flags[bx, by : by + 1, :].astype(jnp.float32), (SUB, flags.shape[2])
                    ),
                    flag_z[...],
                )
                for by in range(2)
            ],
            axis=0,
        )
        rows = [ext_x[0, 3 + bx * SUB + i] for i in range(SUB)]
        for power in range(4):
            total = jnp.zeros((cy, cz), jnp.float32)
            for i in range(SUB):
                total = total + rows[i] * (((i + 0.5) / SUB - 0.5) ** power)
            rows_p[pl.ds((bx * 4 + power) * 2 * SUB, 2 * SUB), :] = total * flagged
    weighted = contract_rows(rows_p[...], spread[...]) * along_z[...]
    shifted = exact(cell_rows[...], weighted)

    def choose(stack, lanes):
        lane = lax.rem(lax.broadcasted_iota(jnp.int32, (8, lanes), 1), slot)
        total = jnp.zeros((8, lanes), jnp.float32)
        for sd in range(6):
            inside = (lane >= sd * count_m) & (lane < (sd + 1) * count_m)
            total = total + jnp.where(inside, stack[sd * 8 : sd * 8 + 8], 0.0)
        return total

    block = choose(shifted, 4 * slot)
    near[1, 1] = block
    first = exact(block, pick_up[...])
    tile = choose(exact(one_rows[...], first), slot)
    px, py = lax.rem(mx, 2), lax.rem(my, 2)
    lifted = exact(first, second[px * 2 + py])
    for dz in range(2):
        part = exact(two_rows[dz * 48 : dz * 48 + 48], lifted[:, dz * slot : (dz + 1) * slot])
        tile = tile + choose(part, slot)
    row_index = lax.broadcasted_iota(jnp.int32, (8, slot), 0)
    tiles[mx, my] = jnp.where(row_index == 7, best, tile)

    for step in range(1, count_y):
        remote(
            tiles.at[mx, my], tiles.at[mx, my],
            first_send.at[step], first_recv.at[step], at_y(step),
        ).start()
    side_y = (
        remote(near.at[1, 1], near.at[1, 2], side_send.at[0], side_recv.at[0], at_y(-1)),
        remote(near.at[1, 1], near.at[1, 0], side_send.at[1], side_recv.at[1], at_y(1)),
    )
    start_halo(side_y, my, count_y)

    lane_z = lax.broadcasted_iota(jnp.int32, (cy, cz), 1)

    def pack(row, carry):
        mine = (lane_z >= row * 8) & (lane_z < row * 8 + 8)
        for field in range(nf):
            turned = pltpu.roll(ext_x[field, 3 + row], row * 8 + 3, 1)
            packed[field] = jnp.where(mine, turned, packed[field])
        return carry

    packed[...] = jnp.ones(packed.shape, jnp.float32)
    lax.fori_loop(0, cx, pack, 0)

    def end_stencil(field):
        value = packed[field]
        one = pltpu.roll(value, cz - 1, 1)
        two = pltpu.roll(value, cz - 2, 1)
        return value, one, two, two, two, two

    def end_emit(field, flux):
        packed_flux[field] = flux

    emit_fluxes(end_stencil, 2, nf, end_emit)

    def sweep_z(row, carry):
        def stencil(field):
            value = ext_x[field, 3 + row]
            first_lane = value[:, 0:1]
            last_lane = value[:, cz - 1 : cz]
            out = []
            for step in range(-3, 3):
                if step == 0:
                    out.append(value)
                elif step < 0:
                    out.append(jnp.where(lane_z < -step, first_lane, pltpu.roll(value, -step, 1)))
                else:
                    out.append(
                        jnp.where(lane_z >= cz - step, last_lane, pltpu.roll(value, cz - step, 1))
                    )
            return out

        def emit(field, flux):
            ending = pltpu.roll(packed_flux[field], cz - 1 - row * 8, 1)
            above = jnp.where(lane_z == cz - 1, ending, pltpu.roll(flux, cz - 1, 1))
            section[field, row] = above - flux

        emit_fluxes(stencil, 2, nf, emit)
        return carry

    lax.fori_loop(0, cx, sweep_z, 0)

    for step in range(1, count_y):
        arrived = tiles.at[mx, lax.rem(my - step + count_y, count_y)]
        copy = remote(arrived, arrived, first_send.at[step], first_recv.at[step], at_y(step))
        copy.wait_send()
        copy.wait_recv()

    def finish_side(pair, position, count, low, high):
        @pl.when(position > 0)
        def _():
            pair[0].wait_send()
            pair[1].wait_recv()

        @pl.when(position < count - 1)
        def _():
            pair[1].wait_send()
            pair[0].wait_recv()

        @pl.when(position == 0)
        def _():
            low[...] = jnp.zeros(low.shape, jnp.float32)

        @pl.when(position == count - 1)
        def _():
            high[...] = jnp.zeros(high.shape, jnp.float32)

    finish_side(side_y, my, count_y, near.at[1, 0], near.at[1, 2])
    for step in range(1, count_x):
        remote(
            tiles.at[mx], tiles.at[mx], second_send.at[step], second_recv.at[step], at_x(step)
        ).start()
    side_x = (
        remote(near.at[1], near.at[2], side_send.at[2], side_recv.at[2], at_x(-1)),
        remote(near.at[1], near.at[0], side_send.at[3], side_recv.at[3], at_x(1)),
    )
    start_halo(side_x, mx, count_x)

    def sweep(buffer, length, direction, store):
        def stencil_at(face):
            return lambda field: [buffer[field, face + i] for i in range(6)]

        def start_emit(field, flux):
            previous[field] = flux

        emit_fluxes(stencil_at(0), direction, nf, start_emit)

        def body(cell, carry):
            def emit(field, flux):
                store(field, cell, flux - previous[field])
                previous[field] = flux

            emit_fluxes(stencil_at(cell + 1), direction, nf, emit)
            return carry

        lax.fori_loop(0, length, body, 0)

    finish_halo(pair_y, ext_y, cy, my, count_y)

    def store_y(field, cell, value):
        moved[field, cell] = value

    sweep(ext_y, cy, 1, store_y)

    for step in range(1, count_x):
        arrived = tiles.at[lax.rem(mx - step + count_x, count_x)]
        copy = remote(arrived, arrived, second_send.at[step], second_recv.at[step], at_x(step))
        copy.wait_send()
        copy.wait_recv()
    finish_side(side_x, mx, count_x, near.at[0], near.at[2])

    fastest = jnp.max(jnp.max(tiles[...], axis=(0, 1))[7:8, :])
    step_size = courant / (SUB * jnp.full((1, cz), fastest, jnp.float32))

    one_x, one_y = mx // 2, my // 2
    two_x, two_y = mx // 4, my // 4

    def united(ux, uy):
        return (
            tiles[2 * ux, 2 * uy] + tiles[2 * ux, 2 * uy + 1]
            + tiles[2 * ux + 1, 2 * uy] + tiles[2 * ux + 1, 2 * uy + 1]
        )

    def held(value, count):
        return jnp.clip(value, 0, count - 1), (value >= 0) & (value < count)

    for dx in range(3):
        for dy in range(3):
            base = (dx * 3 + dy) * 4 * slot
            window[0:8, base : base + 4 * slot] = near[dx, dy]
            for bx in range(2):
                for by in range(2):
                    at = base + (bx * 2 + by) * slot
                    gx, in_x = held(2 * (one_x + dx - 1) + bx, count_x)
                    gy, in_y = held(2 * (one_y + dy - 1) + by, count_y)
                    ux, in_ux = held(2 * (two_x + dx - 1) + bx, count_x // 2)
                    uy, in_uy = held(2 * (two_y + dy - 1) + by, count_y // 2)
                    own = jnp.where(in_x & in_y, tiles[gx, gy], 0.0)
                    joint = jnp.where(in_ux & in_uy, united(ux, uy), 0.0)
                    window[8:16, at : at + slot] = jnp.where(
                        row_index < 4, own, jnp.where(row_index < 6, joint, 0.0)
                    )

    for copy in tables:
        copy.wait()

    def tripled(left, high, low):
        left_high = left.astype(jnp.bfloat16)
        left_low = (left - left_high.astype(jnp.float32)).astype(jnp.bfloat16)
        both = jnp.concatenate([left_high, left_low], axis=0)
        wide_part = jnp.dot(both, high, preferred_element_type=jnp.float32)
        size = left.shape[0]
        return (
            wide_part[:size] + wide_part[size:]
            + jnp.dot(left_high, low, preferred_element_type=jnp.float32)
        )

    sums = tripled(window[...], mid_hi[...], mid_lo[...]) * scale[...]
    inner = jnp.concatenate(
        [window[:, column * slot : (column + 1) * slot] for column in inner_columns], axis=1
    )
    touching = tripled(inner, cls_hi[...], cls_lo[...])

    def select(values, which):
        total = jnp.zeros((values.shape[0], 64), jnp.float32)
        for child in range(4):
            total = total + jnp.where(which == child, values[:, child * 64 : child * 64 + 64], 0.0)
        return total

    lane_64 = lax.broadcasted_iota(jnp.int32, (8, 64), 1)
    same_half = (lane_64 >= 32) == (lax.rem(lax.broadcasted_iota(jnp.int32, (8, 64), 0), 2) == 1)
    which_two = lax.rem(one_x, 2) * 2 + lax.rem(one_y, 2)
    second_sum = select(sums, which_two)
    if top:
        nx3, ny3 = count_x // 4, count_y // 4
        grown = jnp.zeros((8, slot), jnp.float32)
        for sx in range(nx3):
            for sy in range(ny3):
                source = jnp.zeros((8, slot), jnp.float32)
                for bx in range(2):
                    for by in range(2):
                        source = source + exact(
                            united(2 * sx + bx, 2 * sy + by), raise_up[bx * 2 + by]
                        )
                source = jnp.where((row_index == 4) | (row_index == 5), source, 0.0)
                place = ((sx - two_x + nx3 - 1) * (2 * ny3 - 1) + (sy - two_y + ny3 - 1)) * 3
                for dz in range(3):
                    moved_rows = source if dz == 1 else pltpu.roll(source, 1 if dz == 0 else 7, 0)
                    grown = grown + exact(moved_rows, far[place + dz])
        grown = jnp.where((row_index == 4) | (row_index == 5), grown, 0.0)
        carried = exact(grown, lower_down[which_two])
        second_sum = second_sum + jnp.concatenate([jnp.zeros((8, 64), jnp.float32), carried], axis=0)
    from_two = jnp.where(same_half, exact(take_two[...], second_sum), 0.0)
    first_sum = exact(take_one[...], select(sums, px * 2 + py)) + exact(
        from_two, down_two[px * 2 + py]
    )
    from_one = jnp.where(same_half, exact(take_zero[...], first_sum), 0.0)
    expansion = sums[0:8] + touching[0:8] + exact(from_one, down_one[...])
    on_z = contract_rows(expansion, to_z[...])
    for k in range(3):
        parts = exact(fields[k], on_z * weights[1 if k == 2 else 0])
        for row in range(cx):
            bx, height = row // SUB, (row % SUB + 0.5) / SUB - 0.5
            base = bx * 6 * SUB
            accel[k, row] = (
                parts[base : base + 2 * SUB]
                + height * parts[base + 2 * SUB : base + 4 * SUB]
                + (height * height) * parts[base + 4 * SUB : base + 6 * SUB]
            )

    finish_halo(pair_x, ext_x, cx, mx, count_x)

    def store_x(field, cell, value):
        total = (value + section[field, cell] + moved[field, :, cell, :]) * (-float(SUB))
        if 1 <= field <= 3:
            total = total + ext_x[0, 3 + cell] * accel[field - 1, cell]
        if field == 4:
            for k in range(3):
                total = total + ext_x[1 + k, 3 + cell] * accel[k, cell]
        section[field, cell] = ext_x[field, 3 + cell] + step_size * total

    sweep(ext_x, cx, 0, store_x)


def shards(density, momentum, energy, entropy, tracers, leaf_flags):
    count_x, count_y = lax.axis_size("mx"), lax.axis_size("my")
    cx, cy, cz = density.shape
    nf = 6 + tracers.shape[0]
    middle, close = window_tables()
    top, raise_up, lower_down, far = top_tables(count_x // 4, count_y // 4)
    constants = [
        *split_pair(middle),
        *split_pair(close),
        *[jnp.asarray(t, jnp.float32) for t in moment_tables(cz)],
        *[jnp.asarray(t, jnp.float32) for t in down_tables(cz)],
        *[jnp.asarray(t, jnp.float32) for t in (raise_up, lower_down, far)],
    ]
    anywhere = pl.BlockSpec(memory_space=pl.ANY)
    local = pl.BlockSpec(memory_space=pltpu.VMEM)
    dma = pltpu.SemaphoreType.DMA
    f32 = jnp.float32
    return pl.pallas_call(
        functools.partial(section_kernel, (count_x, count_y, nf, cx, cy, cz), top),
        out_shape=(
            jax.ShapeDtypeStruct((nf, cx, cy, cz), f32),
            jax.ShapeDtypeStruct((3, cx, cy, cz), f32),
        ),
        in_specs=[anywhere] * 5 + [local] + [anywhere] * 4 + [local] * (len(constants) - 4),
        out_specs=(local, local),
        scratch_shapes=[
            pltpu.VMEM((nf, cx + 6, cy, cz), f32),
            pltpu.VMEM((nf, cy + 6, cx, cz), f32),
            pltpu.VMEM((nf, cy, cx, cz), f32),
            pltpu.VMEM((nf, cy, cz), f32),
            pltpu.VMEM((nf, cy, cz), f32),
            pltpu.VMEM((nf, cy, cz), f32),
            pltpu.VMEM((count_x, count_y, 8, slot), f32),
            pltpu.VMEM((3, 3, 8, 4 * slot), f32),
            pltpu.VMEM((16, 36 * slot), f32),
            pltpu.VMEM((128, cz), f32),
            pltpu.VMEM(middle.shape, jnp.bfloat16),
            pltpu.VMEM(middle.shape, jnp.bfloat16),
            pltpu.VMEM(close.shape, jnp.bfloat16),
            pltpu.VMEM(close.shape, jnp.bfloat16),
            dma((5,)), dma((4,)), dma((4,)), dma((4,)),
            dma((count_y,)), dma((count_y,)), dma((count_x,)), dma((count_x,)),
            dma((4,)), dma((4,)),
        ],
        compiler_params=pltpu.CompilerParams(
            collective_id=0, has_side_effects=True, vmem_limit_bytes=56 * 1024 * 1024
        ),
    )(density[None], momentum, energy[None], entropy[None], tracers, leaf_flags, *constants)


def solution(mesh):
    placed = (
        P("mx", "my", None),
        P(None, "mx", "my", None),
        P("mx", "my", None),
        P("mx", "my", None),
        P(None, "mx", "my", None),
        P("mx", "my", None),
    )
    return jax.shard_map(
        shards,
        mesh=mesh,
        in_specs=placed,
        out_specs=(P(None, "mx", "my", None), P(None, "mx", "my", None)),
        check_vma=False,
    )
```

time: 1120 us -> 44.8 us (0.04)
  local copies, waits for them, and re-layouts: 457 us -> 3.79 us
  other arithmetic: 437 us -> 0 us
  blocking collectives: 109 us -> 0 us
  loops' own time: 57.2 us -> 0 us
  Pallas kernels: 0 us -> 40.2 us
  starting transfers between devices: 24.2 us -> 0 us
  matrix products: 22.2 us -> 0 us
    while x672 -> x0, other arithmetic: 252 us -> none
    while x855 -> x0, local copies, waits for them, and re-layouts: 225 us -> none
    mul x162 -> x0, other arithmetic: 90.6 us -> none  [the longest x147 82.6 us: visit(): pieces.append(piece * weight[None])]
    all_gather x1 -> x0, blocking collectives: 68.8 us -> none  [gravity_local(): gathered = lax.all_gather(first_level, ('mx', 'my'), axis=1, tiled=True)]
    reshape x53 -> x0, local copies, waits for them, and re-layouts: 64.6 us -> none  [the longest x24 49.5 us: visit(): jnp.stack(pieces, axis=0).reshape(inner_count * moments_count, cells_count)]
    another operation x4 -> x0, loops' own time: 57.2 us -> none  [local_from_far(): running, _ = lax.scan(visit, initial, (grouped_kernels, shifts))]
    another operation x220 -> x0, local copies, waits for them, and re-layouts: 52 us -> none  [visit(): jnp.stack(pieces, axis=0).reshape(inner_count * moments_count, cells_count)]
    pallas_call x0 -> x1, Pallas kernels: none -> 40.2 us  [shards(): pl.pallas_call(functools.partial(section_kernel, (count_x, count_y, nf, c...]
  transfers between devices with their start and end apart: 8 -> 0, of which waited for: 0 -> 0; matrix products, arithmetic and copies ran while one was open for 78% -> 0% of each run, Pallas kernels for 0% -> 0%
where the time goes in v1:
time: 44.8 us; the launch traced here: 44.6 us
  Pallas kernels  40.2 us (90%)
  local copies, waits for them, and re-layouts  3.79 us (8%)
  between operations  0.65 us (1%)
    pallas_call x1, Pallas kernels, shards(): pl.pallas_call(functools.partial(section_kernel, (count_x, count_y, nf, c...  40.2 us
    unnamed x4, local copies, waits for them, and re-layouts  3.79 us

profile of v1, /device:TPU:0, one launch (start us, length us, event | category | flops | bytes accessed | tf_op | source)
XLA Modules:
  0.0 44.6 jit_solution(8777561812481861388)
XLA Ops:
  0.6 40.2 %shard_map.275 = (f32[15,16,16,128]{3,2,1,0:T(8,128)}, f32[3,16,16,128]{3,2,1,0:T(8,128)}) custom-call(f32[1,16,16,128]{3,2,1,0:T(8,128)} %bitcast.3, f32[3,16,16,128]{3,2,1,0:T(8,128)} %momentum.1, f32[1,16,16,128]{3,2,1,0:T(8,128)} %bitcast.4, f32[1,16,16,128]{3,2,1,0:T(8,128)} %bitcast.5, f32[9,16,16,128]{3,2,1,0:T(8,128)} %tracers.1, s32[2,2,16]{2,1,0:T(2,128)} %flags.1, ...), custom_call_target="tpu_custom_call" | custom-call | tf_op jit(solution)/shard_map/pallas_call | solution.py:781
  40.8 0.0 copy-start
  40.8 3.0 %copy.32 = f32[15,16,16,128]{3,2,1,0:T(8,128)} copy(f32[15,16,16,128]{3,2,1,0:T(8,128)} %get-tuple-element.4) | data formatting | bytes 3932160
  43.9 0.0 copy-done
  43.9 0.7 %copy.33 = f32[3,16,16,128]{3,2,1,0:T(8,128)} copy(f32[3,16,16,128]{3,2,1,0:T(8,128)S(1)} %copy-done) | data formatting | bytes 786432
Async XLA Ops:
  40.8 3.1 %copy-start = (f32[3,16,16,128]{3,2,1,0:T(8,128)S(1)}, f32[3,16,16,128]{3,2,1,0:T(8,128)}, u32[]{:S(2)}) copy-start(f32[3,16,16,128]{3,2,1,0:T(8,128)} %get-tuple-element.5) | copy-start | bytes 1179652

commit v2 on v1

--- a/solution.py
+++ b/solution.py
@@ -337,7 +337,7 @@
     return left, right
 
 
-def emit_fluxes(stencil_of, direction, count_fields, emit):
+def prepare(stencil_of, direction):
     mass = states_of(stencil_of(0))
     push = states_of(stencil_of(1 + direction))
     heat = states_of(stencil_of(5))
@@ -345,17 +345,22 @@
     speed = [push[i] * inverse[i] for i in range(2)]
     gas = [sound(heat[i], inverse[i]) for i in range(2)]
     fastest = jnp.maximum(jnp.abs(speed[0]) + gas[0][1], jnp.abs(speed[1]) + gas[1][1])
-    weight_left = 0.5 * (speed[0] + fastest)
-    weight_right = 0.5 * (speed[1] - fastest)
+    weights = 0.5 * (speed[0] + fastest), 0.5 * (speed[1] - fastest)
+    flux = [left * weights[0] + right * weights[1] for left, right in (mass, push, heat)]
+    flux[1] = flux[1] + 0.5 * (gas[0][0] + gas[1][0])
+    work = 0.5 * (gas[0][0] * speed[0] + gas[1][0] * speed[1])
+    return (*flux, *weights, work)
+
+
+def apply(prepared, stencil_of, direction, count_fields, emit):
+    known = dict(zip((0, 1 + direction, 5), prepared[:3]))
     for field in range(count_fields):
-        known = {0: mass, 1 + direction: push, 5: heat}
-        left, right = known[field] if field in known else states_of(stencil_of(field))
-        flux = left * weight_left + right * weight_right
-        if field == 1 + direction:
-            flux = flux + 0.5 * (gas[0][0] + gas[1][0])
-        if field == 4:
-            flux = flux + 0.5 * (gas[0][0] * speed[0] + gas[1][0] * speed[1])
-        emit(field, flux)
+        if field in known:
+            emit(field, known[field])
+            continue
+        left, right = states_of(stencil_of(field))
+        flux = left * prepared[3] + right * prepared[4]
+        emit(field, flux + prepared[5] if field == 4 else flux)
 
 
 def section_kernel(
@@ -401,7 +406,6 @@
         pl.semaphore_signal(barrier, inc=1, device_id=at_x(step), device_id_type=MESH)
     for step in range(1, count_y):
         pl.semaphore_signal(barrier, inc=1, device_id=at_y(step), device_id_type=MESH)
-    pl.semaphore_wait(barrier, count_x + count_y - 2)
     for copy in loads:
         copy.wait()
 
@@ -461,19 +465,22 @@
         return carry
 
     lax.fori_loop(0, nf, turn, 0)
+    pl.semaphore_wait(barrier, count_x + count_y - 2)
     start_halo(pair_y, my, count_y)
     start_halo(pair_x, mx, count_x)
 
-    def cell_speed(row, best):
-        inverse = 1.0 / ext_x[0, 3 + row]
+    planes = 4
+
+    def cell_speed(step, best):
+        rows = pl.ds(3 + step * planes, planes)
+        inverse = 1.0 / ext_x[0, rows]
         largest = jnp.maximum(
-            jnp.maximum(jnp.abs(ext_x[1, 3 + row]), jnp.abs(ext_x[2, 3 + row])),
-            jnp.abs(ext_x[3, 3 + row]),
-        )
-        _, speed = sound(ext_x[5, 3 + row], inverse)
-        return jnp.maximum(best, largest * inverse + speed)
-
-    best = lax.fori_loop(0, cx, cell_speed, jnp.zeros((cy, cz), jnp.float32))
+            jnp.maximum(jnp.abs(ext_x[1, rows]), jnp.abs(ext_x[2, rows])), jnp.abs(ext_x[3, rows])
+        )
+        _, speed = sound(ext_x[5, rows], inverse)
+        return jnp.maximum(best, jnp.max(largest * inverse + speed, axis=0))
+
+    best = lax.fori_loop(0, cx // planes, cell_speed, jnp.zeros((cy, cz), jnp.float32))
     best = jnp.max(best)
 
     for bx in range(2):
@@ -550,34 +557,32 @@
     def end_emit(field, flux):
         packed_flux[field] = flux
 
-    emit_fluxes(end_stencil, 2, nf, end_emit)
-
-    def sweep_z(row, carry):
+    apply(prepare(end_stencil, 2), end_stencil, 2, nf, end_emit)
+
+    def stencil_z(row):
         def stencil(field):
             value = ext_x[field, 3 + row]
-            first_lane = value[:, 0:1]
-            last_lane = value[:, cz - 1 : cz]
-            out = []
-            for step in range(-3, 3):
-                if step == 0:
-                    out.append(value)
-                elif step < 0:
-                    out.append(jnp.where(lane_z < -step, first_lane, pltpu.roll(value, -step, 1)))
-                else:
-                    out.append(
-                        jnp.where(lane_z >= cz - step, last_lane, pltpu.roll(value, cz - step, 1))
-                    )
+            out = [value]
+            for step in range(3):
+                out.insert(0, jnp.where(lane_z < 1, value, pltpu.roll(out[0], 1, 1)))
+            for step in range(2):
+                out.append(jnp.where(lane_z == cz - 1, value, pltpu.roll(out[-1], cz - 1, 1)))
             return out
+
+        return stencil
+
+    def sweep_z(row, prepared):
+        following = prepare(stencil_z(jnp.minimum(row + 1, cx - 1)), 2)
 
         def emit(field, flux):
             ending = pltpu.roll(packed_flux[field], cz - 1 - row * 8, 1)
             above = jnp.where(lane_z == cz - 1, ending, pltpu.roll(flux, cz - 1, 1))
             section[field, row] = above - flux
 
-        emit_fluxes(stencil, 2, nf, emit)
-        return carry
-
-    lax.fori_loop(0, cx, sweep_z, 0)
+        apply(prepared, stencil_z(row), 2, nf, emit)
+        return following
+
+    lax.fori_loop(0, cx, sweep_z, prepare(stencil_z(0), 2))
 
     for step in range(1, count_y):
         arrived = tiles.at[mx, lax.rem(my - step + count_y, count_y)]
@@ -622,17 +627,19 @@
         def start_emit(field, flux):
             previous[field] = flux
 
-        emit_fluxes(stencil_at(0), direction, nf, start_emit)
-
-        def body(cell, carry):
+        apply(prepare(stencil_at(0), direction), stencil_at(0), direction, nf, start_emit)
+
+        def body(cell, prepared):
+            following = prepare(stencil_at(jnp.minimum(cell + 2, length)), direction)
+
             def emit(field, flux):
                 store(field, cell, flux - previous[field])
                 previous[field] = flux
 
-            emit_fluxes(stencil_at(cell + 1), direction, nf, emit)
-            return carry
-
-        lax.fori_loop(0, length, body, 0)
+            apply(prepared, stencil_at(cell + 1), direction, nf, emit)
+            return following
+
+        lax.fori_loop(0, length, body, prepare(stencil_at(1), direction))
 
     finish_halo(pair_y, ext_y, cy, my, count_y)
 

time: 44.8 us -> 37.7 us (0.84)
  Pallas kernels: 40.2 us -> 33.1 us
    pallas_call x1, Pallas kernels: 40.2 us -> 33.1 us  [shards(): pl.pallas_call(functools.partial(section_kernel, (count_x, count_y, nf, c...]
where the time goes in v2:
time: 37.7 us; the launch traced here: 37.5 us
  Pallas kernels  33.1 us (88%)
  local copies, waits for them, and re-layouts  3.79 us (10%)
  between operations  0.65 us (2%)
    pallas_call x1, Pallas kernels, shards(): pl.pallas_call(functools.partial(section_kernel, (count_x, count_y, nf, c...  33.1 us
    unnamed x4, local copies, waits for them, and re-layouts  3.79 us

profile of v2, /device:TPU:0, one launch (start us, length us, event | category | flops | bytes accessed | tf_op | source)
XLA Modules:
  0.0 37.5 jit_solution(10541399524218447218)
XLA Ops:
  0.6 33.1 %shard_map.275 = (f32[15,16,16,128]{3,2,1,0:T(8,128)}, f32[3,16,16,128]{3,2,1,0:T(8,128)}) custom-call(f32[1,16,16,128]{3,2,1,0:T(8,128)} %bitcast.3, f32[3,16,16,128]{3,2,1,0:T(8,128)} %momentum.1, f32[1,16,16,128]{3,2,1,0:T(8,128)} %bitcast.4, f32[1,16,16,128]{3,2,1,0:T(8,128)} %bitcast.5, f32[9,16,16,128]{3,2,1,0:T(8,128)} %tracers.1, s32[2,2,16]{2,1,0:T(2,128)} %flags.1, ...), custom_call_target="tpu_custom_call" | custom-call | tf_op jit(solution)/shard_map/pallas_call | solution.py:788
  33.7 0.0 copy-start
  33.7 3.0 %copy.32 = f32[15,16,16,128]{3,2,1,0:T(8,128)} copy(f32[15,16,16,128]{3,2,1,0:T(8,128)} %get-tuple-element.4) | data formatting | bytes 3932160
  36.8 0.0 copy-done
  36.8 0.7 %copy.33 = f32[3,16,16,128]{3,2,1,0:T(8,128)} copy(f32[3,16,16,128]{3,2,1,0:T(8,128)S(1)} %copy-done) | data formatting | bytes 786432
Async XLA Ops:
  33.7 3.1 %copy-start = (f32[3,16,16,128]{3,2,1,0:T(8,128)S(1)}, f32[3,16,16,128]{3,2,1,0:T(8,128)}, u32[]{:S(2)}) copy-start(f32[3,16,16,128]{3,2,1,0:T(8,128)} %get-tuple-element.5) | copy-start | bytes 1179652

commit v3 on v2

--- a/solution.py
+++ b/solution.py
@@ -147,6 +147,12 @@
     for by in range(2)
     if 1 <= 2 * dx + bx <= 4 and 1 <= 2 * dy + by <= 4
 ]
+
+
+early_names = (
+    "flag_z", "cell_rows", "along_z", "spread_hi", "spread_lo", "pick_up_hi", "pick_up_lo",
+    "second_hi", "second_lo", "one_rows", "two_rows",
+)
 
 
 def split_pair(table):
@@ -312,15 +318,30 @@
     return bool(counting.any()), raise_up, lower_down, far
 
 
-def exact(left, right):
+def halves(value):
+    high = value.astype(jnp.bfloat16)
+    return high, (value - high.astype(jnp.float32)).astype(jnp.bfloat16)
+
+
+def product(left, right):
+    return jnp.dot(left, right, preferred_element_type=jnp.float32)
+
+
+def times(value, table_hi, table_lo):
+    high, low = halves(value)
+    size = value.shape[0]
+    both = product(jnp.concatenate([high, low], axis=0), table_hi)
+    return both[:size] + both[size:] + product(high, table_lo)
+
+
+def wholly(left, right):
     return jnp.dot(left, right, precision=highest, preferred_element_type=jnp.float32)
 
 
-def contract_rows(left, right):
-    return lax.dot_general(
-        left, right, (((0,), (0,)), ((), ())), precision=highest,
-        preferred_element_type=jnp.float32,
-    )
+def picked(zero_one, value):
+    high, low = halves(value)
+    pick = zero_one.astype(jnp.bfloat16)
+    return product(pick, high) + product(pick, low)
 
 
 def sound(entropy, inverse):
@@ -364,18 +385,16 @@
 
 
 def section_kernel(
-    sizes, top,
-    density, momentum, energy, entropy, tracers, flags,
-    middle_hi, middle_lo, close_hi, close_lo,
-    spread, along_z, cell_rows, pick_up, one_rows, second, two_rows, flag_z,
-    scale, down_two, down_one, take_one, take_two, take_zero, to_z, weights, fields,
-    raise_up, lower_down, far,
-    section, accel,
-    ext_x, ext_y, moved, previous, packed, packed_flux, tiles, near, window, rows_p,
-    mid_hi, mid_lo, cls_hi, cls_lo,
-    load_sem, table_sem, halo_send, halo_recv, first_send, first_recv,
-    second_send, second_recv, side_send, side_recv,
+    sizes, top, names, density, momentum, energy, entropy, tracers, flags, *rest
 ):
+    held_tables = dict(zip(names, rest[: len(names)]))
+    section, accel = rest[len(names) : len(names) + 2]
+    table = dict(zip(names, rest[len(names) + 2 : 2 * len(names) + 2]))
+    (
+        ext_x, ext_y, moved, previous, packed, packed_flux, tiles, near, window, rows_p, splits,
+        load_sem, table_sem, halo_send, halo_recv, first_send, first_recv,
+        second_send, second_recv, side_send, side_recv,
+    ) = rest[2 * len(names) + 2 :]
     count_x, count_y, nf, cx, cy, cz = sizes
     mx, my = lax.axis_index("mx"), lax.axis_index("my")
     loads = [
@@ -384,15 +403,16 @@
             [(density, 0, 1), (momentum, 1, 3), (energy, 4, 1), (entropy, 5, 1), (tracers, 6, nf - 6)]
         )
     ]
-    tables = [
-        pltpu.make_async_copy(source, target, table_sem.at[i])
-        for i, (source, target) in enumerate(
-            [(middle_hi, mid_hi), (middle_lo, mid_lo), (close_hi, cls_hi), (close_lo, cls_lo)]
-        )
-    ]
+    px, py = lax.rem(mx, 2), lax.rem(my, 2)
+    tables = {}
+    for i, name in enumerate(names):
+        source = held_tables[name]
+        if name.startswith("second"):
+            source = source.at[px * 2 + py]
+        tables[name] = pltpu.make_async_copy(source, table[name], table_sem.at[i])
     for copy in loads:
         copy.start()
-    for copy in tables:
+    for copy in tables.values():
         copy.start()
 
     def at_x(step):
@@ -483,27 +503,32 @@
     best = lax.fori_loop(0, cx // planes, cell_speed, jnp.zeros((cy, cz), jnp.float32))
     best = jnp.max(best)
 
-    for bx in range(2):
-        flagged = jnp.concatenate(
+    for name in early_names:
+        tables[name].wait()
+    flagged = product(
+        jnp.concatenate(
             [
-                exact(
-                    jnp.broadcast_to(
-                        flags[bx, by : by + 1, :].astype(jnp.float32), (SUB, flags.shape[2])
-                    ),
-                    flag_z[...],
+                jnp.broadcast_to(
+                    flags[bx, by : by + 1, :].astype(jnp.float32), (SUB, flags.shape[2])
                 )
+                for bx in range(2)
                 for by in range(2)
             ],
             axis=0,
-        )
+        ).astype(jnp.bfloat16),
+        table["flag_z"][...].astype(jnp.bfloat16),
+    )
+    for bx in range(2):
         rows = [ext_x[0, 3 + bx * SUB + i] for i in range(SUB)]
         for power in range(4):
-            total = jnp.zeros((cy, cz), jnp.float32)
-            for i in range(SUB):
+            total = rows[0] * ((0.5 / SUB - 0.5) ** power)
+            for i in range(1, SUB):
                 total = total + rows[i] * (((i + 0.5) / SUB - 0.5) ** power)
-            rows_p[pl.ds((bx * 4 + power) * 2 * SUB, 2 * SUB), :] = total * flagged
-    weighted = contract_rows(rows_p[...], spread[...]) * along_z[...]
-    shifted = exact(cell_rows[...], weighted)
+            rows_p[pl.ds((bx * 4 + power) * 2 * SUB, 2 * SUB), :] = (
+                total * flagged[bx * 2 * SUB : (bx + 1) * 2 * SUB]
+            )
+    weighted = times(rows_p[...].T, table["spread_hi"][...], table["spread_lo"][...])
+    shifted = picked(table["cell_rows"][...], weighted * table["along_z"][...])
 
     def choose(stack, lanes):
         lane = lax.rem(lax.broadcasted_iota(jnp.int32, (8, lanes), 1), slot)
@@ -515,12 +540,13 @@
 
     block = choose(shifted, 4 * slot)
     near[1, 1] = block
-    first = exact(block, pick_up[...])
-    tile = choose(exact(one_rows[...], first), slot)
-    px, py = lax.rem(mx, 2), lax.rem(my, 2)
-    lifted = exact(first, second[px * 2 + py])
+    first = times(block, table["pick_up_hi"][...], table["pick_up_lo"][...])
+    tile = choose(picked(table["one_rows"][...], first), slot)
+    lifted = times(first, table["second_hi"][...], table["second_lo"][...])
     for dz in range(2):
-        part = exact(two_rows[dz * 48 : dz * 48 + 48], lifted[:, dz * slot : (dz + 1) * slot])
+        part = picked(
+            table["two_rows"][dz * 48 : dz * 48 + 48], lifted[:, dz * slot : (dz + 1) * slot]
+        )
         tile = tile + choose(part, slot)
     row_index = lax.broadcasted_iota(jnp.int32, (8, slot), 0)
     tiles[mx, my] = jnp.where(row_index == 7, best, tile)
@@ -582,7 +608,7 @@
         apply(prepared, stencil_z(row), 2, nf, emit)
         return following
 
-    lax.fori_loop(0, cx, sweep_z, prepare(stencil_z(0), 2))
+    half_way = lax.fori_loop(0, cx // 2, sweep_z, prepare(stencil_z(0), 2))
 
     for step in range(1, count_y):
         arrived = tiles.at[mx, lax.rem(my - step + count_y, count_y)]
@@ -620,7 +646,9 @@
     )
     start_halo(side_x, mx, count_x)
 
-    def sweep(buffer, length, direction, store):
+    lax.fori_loop(cx // 2, cx, sweep_z, half_way)
+
+    def sweep(buffer, length, direction, store, beside=None, total=(), parts=0):
         def stencil_at(face):
             return lambda field: [buffer[field, face + i] for i in range(6)]
 
@@ -629,7 +657,8 @@
 
         apply(prepare(stencil_at(0), direction), stencil_at(0), direction, nf, start_emit)
 
-        def body(cell, prepared):
+        def body(cell, carry):
+            prepared, total = carry
             following = prepare(stencil_at(jnp.minimum(cell + 2, length)), direction)
 
             def emit(field, flux):
@@ -637,16 +666,18 @@
                 previous[field] = flux
 
             apply(prepared, stencil_at(cell + 1), direction, nf, emit)
-            return following
-
-        lax.fori_loop(0, length, body, prepare(stencil_at(1), direction))
-
-    finish_halo(pair_y, ext_y, cy, my, count_y)
-
-    def store_y(field, cell, value):
-        moved[field, cell] = value
-
-    sweep(ext_y, cy, 1, store_y)
+            return following, total
+
+        def fuller(cell, carry):
+            prepared, total = body(cell, carry)
+            for part in range(2):
+                total = beside(cell * 2 + part, total)
+            return prepared, total
+
+        carry = prepare(stencil_at(1), direction), total
+        if parts > 0:
+            carry = lax.fori_loop(0, parts // 2, fuller, carry)
+        return lax.fori_loop(parts // 2, length, body, carry)[1]
 
     for step in range(1, count_x):
         arrived = tiles.at[lax.rem(mx - step + count_x, count_x)]
@@ -687,25 +718,41 @@
                         row_index < 4, own, jnp.where(row_index < 6, joint, 0.0)
                     )
 
-    for copy in tables:
-        copy.wait()
-
-    def tripled(left, high, low):
-        left_high = left.astype(jnp.bfloat16)
-        left_low = (left - left_high.astype(jnp.float32)).astype(jnp.bfloat16)
-        both = jnp.concatenate([left_high, left_low], axis=0)
-        wide_part = jnp.dot(both, high, preferred_element_type=jnp.float32)
-        size = left.shape[0]
+    for name in names:
+        if name not in early_names:
+            tables[name].wait()
+
+    keep = (lax.broadcasted_iota(jnp.int32, (16, wide), 0) < 8).astype(jnp.float32)
+    middle_chunks = 36 * slot // wide
+    chunks = middle_chunks + len(inner_columns) * slot // wide
+    for index in range(chunks):
+        if index < middle_chunks:
+            value = window[:, index * wide : (index + 1) * wide]
+        else:
+            pair = inner_columns[2 * (index - middle_chunks) :][:2]
+            value = keep * jnp.concatenate(
+                [window[:, column * slot : (column + 1) * slot] for column in pair], axis=1
+            )
+        high, low = halves(value)
+        splits[index, 0:16] = high
+        splits[index, 16:32] = low
+
+    finish_halo(pair_y, ext_y, cy, my, count_y)
+
+    def store_y(field, cell, value):
+        moved[field, cell] = value
+
+    def partial_sum(index, total):
+        both = splits[index]
         return (
-            wide_part[:size] + wide_part[size:]
-            + jnp.dot(left_high, low, preferred_element_type=jnp.float32)
-        )
-
-    sums = tripled(window[...], mid_hi[...], mid_lo[...]) * scale[...]
-    inner = jnp.concatenate(
-        [window[:, column * slot : (column + 1) * slot] for column in inner_columns], axis=1
-    )
-    touching = tripled(inner, cls_hi[...], cls_lo[...])
+            total[0] + product(both, table["window_hi"][index]),
+            total[1] + product(both[:16], table["window_lo"][index]),
+        )
+
+    zeros = jnp.zeros((32, wide), jnp.float32), jnp.zeros((16, wide), jnp.float32)
+    upper, lower = sweep(ext_y, cy, 1, store_y, partial_sum, zeros, chunks)
+    sums = (upper[:16] + upper[16:] + lower) * table["scale"][...]
+
 
     def select(values, which):
         total = jnp.zeros((values.shape[0], 64), jnp.float32)
@@ -725,26 +772,35 @@
                 source = jnp.zeros((8, slot), jnp.float32)
                 for bx in range(2):
                     for by in range(2):
-                        source = source + exact(
-                            united(2 * sx + bx, 2 * sy + by), raise_up[bx * 2 + by]
+                        source = source + wholly(
+                            united(2 * sx + bx, 2 * sy + by), table["raise_up"][bx * 2 + by]
                         )
                 source = jnp.where((row_index == 4) | (row_index == 5), source, 0.0)
                 place = ((sx - two_x + nx3 - 1) * (2 * ny3 - 1) + (sy - two_y + ny3 - 1)) * 3
                 for dz in range(3):
                     moved_rows = source if dz == 1 else pltpu.roll(source, 1 if dz == 0 else 7, 0)
-                    grown = grown + exact(moved_rows, far[place + dz])
+                    grown = grown + wholly(moved_rows, table["far"][place + dz])
         grown = jnp.where((row_index == 4) | (row_index == 5), grown, 0.0)
-        carried = exact(grown, lower_down[which_two])
+        carried = wholly(grown, table["lower_down"][which_two])
         second_sum = second_sum + jnp.concatenate([jnp.zeros((8, 64), jnp.float32), carried], axis=0)
-    from_two = jnp.where(same_half, exact(take_two[...], second_sum), 0.0)
-    first_sum = exact(take_one[...], select(sums, px * 2 + py)) + exact(
-        from_two, down_two[px * 2 + py]
+    from_two = jnp.where(same_half, picked(table["take_two"][...], second_sum), 0.0)
+    which_one = px * 2 + py
+    first_sum = picked(table["take_one"][...], select(sums, which_one)) + times(
+        from_two, table["down_two_hi"][which_one], table["down_two_lo"][which_one]
     )
-    from_one = jnp.where(same_half, exact(take_zero[...], first_sum), 0.0)
-    expansion = sums[0:8] + touching[0:8] + exact(from_one, down_one[...])
-    on_z = contract_rows(expansion, to_z[...])
+    from_one = jnp.where(same_half, picked(table["take_zero"][...], first_sum), 0.0)
+    expansion = sums[0:8] + times(from_one, table["down_one_hi"][...], table["down_one_lo"][...])
+    turned_hi, turned_lo = halves(expansion.T)
+    to_z = table["to_z"][...].astype(jnp.bfloat16)
+    on_z = product(turned_hi, to_z) + product(turned_lo, to_z)
+    pieces = []
+    for which, first_row, last_row in ((0, 0, 192), (1, 192, 288)):
+        high, low = halves(on_z * table["weights"][which])
+        field_hi = table["fields_hi"][first_row:last_row]
+        piece = product(field_hi, high) + product(field_hi, low)
+        pieces.append(piece + product(table["fields_lo"][first_row:last_row], high))
     for k in range(3):
-        parts = exact(fields[k], on_z * weights[1 if k == 2 else 0])
+        parts = pieces[0][k * 96 : k * 96 + 96] if k < 2 else pieces[1]
         for row in range(cx):
             bx, height = row // SUB, (row % SUB + 0.5) / SUB - 0.5
             base = bx * 6 * SUB
@@ -774,26 +830,50 @@
     nf = 6 + tracers.shape[0]
     middle, close = window_tables()
     top, raise_up, lower_down, far = top_tables(count_x // 4, count_y // 4)
-    constants = [
-        *split_pair(middle),
-        *split_pair(close),
-        *[jnp.asarray(t, jnp.float32) for t in moment_tables(cz)],
-        *[jnp.asarray(t, jnp.float32) for t in down_tables(cz)],
-        *[jnp.asarray(t, jnp.float32) for t in (raise_up, lower_down, far)],
+    spread, along_z, cell_rows, pick_up, one_rows, second, two_rows, flag_z = moment_tables(cz)
+    scale, down_two, down_one, take_one, take_two, take_zero, to_z, weights, fields = down_tables(cz)
+    constants = {}
+    for name, array in (("flag_z", flag_z), ("cell_rows", cell_rows), ("along_z", along_z)):
+        constants[name] = jnp.asarray(array, jnp.float32)
+    for name, array in (("spread", spread), ("pick_up", pick_up), ("second", second)):
+        constants[name + "_hi"], constants[name + "_lo"] = split_pair(array)
+    for name, array in (("one_rows", one_rows), ("two_rows", two_rows)):
+        constants[name] = jnp.asarray(array, jnp.float32)
+    joined = np.concatenate([middle, close]).reshape(-1, wide, wide)
+    for name, array in (
+        ("window", joined), ("down_two", down_two), ("down_one", down_one),
+        ("fields", fields.reshape(-1, wide)),
+    ):
+        constants[name + "_hi"], constants[name + "_lo"] = split_pair(array)
+    for name, array in (
+        ("scale", scale), ("take_one", take_one), ("take_two", take_two),
+        ("take_zero", take_zero), ("to_z", to_z), ("weights", weights),
+    ):
+        constants[name] = jnp.asarray(array, jnp.float32)
+    if top:
+        for name, array in (("raise_up", raise_up), ("lower_down", lower_down), ("far", far)):
+            constants[name] = jnp.asarray(array, jnp.float32)
+    names = tuple(constants)
+    shapes = [
+        pltpu.VMEM(
+            array.shape[1:] if name.startswith("second") else array.shape, array.dtype
+        )
+        for name, array in constants.items()
     ]
     anywhere = pl.BlockSpec(memory_space=pl.ANY)
     local = pl.BlockSpec(memory_space=pltpu.VMEM)
     dma = pltpu.SemaphoreType.DMA
     f32 = jnp.float32
     return pl.pallas_call(
-        functools.partial(section_kernel, (count_x, count_y, nf, cx, cy, cz), top),
+        functools.partial(section_kernel, (count_x, count_y, nf, cx, cy, cz), top, names),
         out_shape=(
             jax.ShapeDtypeStruct((nf, cx, cy, cz), f32),
             jax.ShapeDtypeStruct((3, cx, cy, cz), f32),
         ),
-        in_specs=[anywhere] * 5 + [local] + [anywhere] * 4 + [local] * (len(constants) - 4),
+        in_specs=[anywhere] * 5 + [local] + [anywhere] * len(names),
         out_specs=(local, local),
-        scratch_shapes=[
+        scratch_shapes=shapes
+        + [
             pltpu.VMEM((nf, cx + 6, cy, cz), f32),
             pltpu.VMEM((nf, cy + 6, cx, cz), f32),
             pltpu.VMEM((nf, cy, cx, cz), f32),
@@ -804,18 +884,15 @@
             pltpu.VMEM((3, 3, 8, 4 * slot), f32),
             pltpu.VMEM((16, 36 * slot), f32),
             pltpu.VMEM((128, cz), f32),
-            pltpu.VMEM(middle.shape, jnp.bfloat16),
-            pltpu.VMEM(middle.shape, jnp.bfloat16),
-            pltpu.VMEM(close.shape, jnp.bfloat16),
-            pltpu.VMEM(close.shape, jnp.bfloat16),
-            dma((5,)), dma((4,)), dma((4,)), dma((4,)),
+            pltpu.VMEM((joined.shape[0], 32, wide), jnp.bfloat16),
+            dma((5,)), dma((len(names),)), dma((4,)), dma((4,)),
             dma((count_y,)), dma((count_y,)), dma((count_x,)), dma((count_x,)),
             dma((4,)), dma((4,)),
         ],
         compiler_params=pltpu.CompilerParams(
             collective_id=0, has_side_effects=True, vmem_limit_bytes=56 * 1024 * 1024
         ),
-    )(density[None], momentum, energy[None], entropy[None], tracers, leaf_flags, *constants)
+    )(density[None], momentum, energy[None], entropy[None], tracers, leaf_flags, *constants.values())
 
 
 def solution(mesh):

time: 37.7 us -> 41.3 us (1.095)
  local copies, waits for them, and re-layouts: 3.79 us -> 5.86 us
  Pallas kernels: 33.1 us -> 34.7 us
    convert_element_type x0 -> x3, local copies, waits for them, and re-layouts: none -> 2.06 us  [split_pair(): return (high, (table - high.astype(jnp.float32)).astype(jnp.bfloat16))]
    pallas_call x1, Pallas kernels: 33.1 us -> 34.7 us  [shards(): pl.pallas_call(functools.partial(section_kernel, (count_x, count_y, nf, c...]
where the time goes in v3:
time: 41.3 us; the launch traced here: 41.2 us
  Pallas kernels  34.7 us (84%)
  local copies, waits for them, and re-layouts  5.86 us (14%)
  between operations  0.65 us (2%)
    pallas_call x1, Pallas kernels, shards(): pl.pallas_call(functools.partial(section_kernel, (count_x, count_y, nf, c...  34.7 us
    unnamed x4, local copies, waits for them, and re-layouts  3.79 us
    convert_element_type x3, local copies, waits for them, and re-layouts, split_pair(): return (high, (table - high.astype(jnp.float32)).astype(jnp.bfloat16))  2.06 us

profile of v3, /device:TPU:0, one launch (start us, length us, event | category | flops | bytes accessed | tf_op | source)
XLA Modules:
  0.0 41.2 jit_solution(4307134538591962047)
XLA Ops:
  0.6 0.7 %broadcast.rest_6_ = bf16[512,128]{1,0:T(8,128)(2,1)} broadcast(bf16[]{:T(256)} %constant.83), dimensions={} | broadcast | bytes 131074 | tf_op jit(solution)/shard_map/convert_element_type | solution.py:161
  1.3 0.7 %broadcast.2.rest_18_ = bf16[288,256]{1,0:T(8,128)(2,1)} broadcast(bf16[]{:T(256)} %constant.83), dimensions={} | broadcast | bytes 147458 | tf_op jit(solution)/shard_map/convert_element_type | solution.py:161
  2.0 0.7 %broadcast.1.rest_8_ = bf16[4,128,256]{2,1,0:T(8,128)(2,1)} broadcast(bf16[]{:T(256)} %constant.83), dimensions={} | broadcast | bytes 262146 | tf_op jit(solution)/shard_map/convert_element_type | solution.py:161
  2.7 34.7 %shard_map.239 = (f32[15,16,16,128]{3,2,1,0:T(8,128)}, f32[3,16,16,128]{3,2,1,0:T(8,128)}) custom-call(f32[1,16,16,128]{3,2,1,0:T(8,128)} %bitcast.3, f32[3,16,16,128]{3,2,1,0:T(8,128)} %momentum.1, f32[1,16,16,128]{3,2,1,0:T(8,128)} %bitcast.4, f32[1,16,16,128]{3,2,1,0:T(8,128)} %bitcast.5, f32[9,16,16,128]{3,2,1,0:T(8,128)} %tracers.1, s32[2,2,16]{2,1,0:T(2,128)} %flags.1, ...), custom_call_target="tpu_custom_call" | custom-call | tf_op jit(solution)/shard_map/pallas_call | solution.py:867
  37.4 0.0 copy-start
  37.4 3.0 %copy.28 = f32[15,16,16,128]{3,2,1,0:T(8,128)} copy(f32[15,16,16,128]{3,2,1,0:T(8,128)} %get-tuple-element.4) | data formatting | bytes 3932160
  40.4 0.0 copy-done
  40.4 0.7 %copy.29 = f32[3,16,16,128]{3,2,1,0:T(8,128)} copy(f32[3,16,16,128]{3,2,1,0:T(8,128)S(1)} %copy-done) | data formatting | bytes 786432
Async XLA Ops:
  37.4 3.1 %copy-start = (f32[3,16,16,128]{3,2,1,0:T(8,128)S(1)}, f32[3,16,16,128]{3,2,1,0:T(8,128)}, u32[]{:S(2)}) copy-start(f32[3,16,16,128]{3,2,1,0:T(8,128)} %get-tuple-element.5) | copy-start | bytes 1179652

commit v4 on v3

--- a/solution.py
+++ b/solution.py
@@ -156,9 +156,10 @@
 
 
 def split_pair(table):
-    table = jnp.asarray(table, jnp.float32)
+    table = np.asarray(table, np.float32)
     high = table.astype(jnp.bfloat16)
-    return high, (table - high.astype(jnp.float32)).astype(jnp.bfloat16)
+    low = (table - high.astype(np.float32)).astype(jnp.bfloat16)
+    return [("_hi", high)] + ([("_lo", low)] if np.any(low.astype(np.float32)) else [])
 
 
 def window_tables():
@@ -331,7 +332,8 @@
     high, low = halves(value)
     size = value.shape[0]
     both = product(jnp.concatenate([high, low], axis=0), table_hi)
-    return both[:size] + both[size:] + product(high, table_lo)
+    both = both[:size] + both[size:]
+    return both if table_lo is None else both + product(high, table_lo)
 
 
 def wholly(left, right):
@@ -503,8 +505,14 @@
     best = lax.fori_loop(0, cx // planes, cell_speed, jnp.zeros((cy, cz), jnp.float32))
     best = jnp.max(best)
 
-    for name in early_names:
-        tables[name].wait()
+    for name in names:
+        if name in early_names:
+            tables[name].wait()
+
+    def pair_of(name, *at):
+        low = name + "_lo"
+        return [table[name + "_hi"][(*at, ...)], table[low][(*at, ...)] if low in names else None]
+
     flagged = product(
         jnp.concatenate(
             [
@@ -527,7 +535,7 @@
             rows_p[pl.ds((bx * 4 + power) * 2 * SUB, 2 * SUB), :] = (
                 total * flagged[bx * 2 * SUB : (bx + 1) * 2 * SUB]
             )
-    weighted = times(rows_p[...].T, table["spread_hi"][...], table["spread_lo"][...])
+    weighted = times(rows_p[...].T, *pair_of("spread"))
     shifted = picked(table["cell_rows"][...], weighted * table["along_z"][...])
 
     def choose(stack, lanes):
@@ -540,9 +548,9 @@
 
     block = choose(shifted, 4 * slot)
     near[1, 1] = block
-    first = times(block, table["pick_up_hi"][...], table["pick_up_lo"][...])
+    first = times(block, *pair_of("pick_up"))
     tile = choose(picked(table["one_rows"][...], first), slot)
-    lifted = times(first, table["second_hi"][...], table["second_lo"][...])
+    lifted = times(first, *pair_of("second"))
     for dz in range(2):
         part = picked(
             table["two_rows"][dz * 48 : dz * 48 + 48], lifted[:, dz * slot : (dz + 1) * slot]
@@ -648,7 +656,7 @@
 
     lax.fori_loop(cx // 2, cx, sweep_z, half_way)
 
-    def sweep(buffer, length, direction, store, beside=None, total=(), parts=0):
+    def sweep(buffer, length, direction, store):
         def stencil_at(face):
             return lambda field: [buffer[field, face + i] for i in range(6)]
 
@@ -657,8 +665,7 @@
 
         apply(prepare(stencil_at(0), direction), stencil_at(0), direction, nf, start_emit)
 
-        def body(cell, carry):
-            prepared, total = carry
+        def body(cell, prepared):
             following = prepare(stencil_at(jnp.minimum(cell + 2, length)), direction)
 
             def emit(field, flux):
@@ -666,18 +673,16 @@
                 previous[field] = flux
 
             apply(prepared, stencil_at(cell + 1), direction, nf, emit)
-            return following, total
-
-        def fuller(cell, carry):
-            prepared, total = body(cell, carry)
-            for part in range(2):
-                total = beside(cell * 2 + part, total)
-            return prepared, total
-
-        carry = prepare(stencil_at(1), direction), total
-        if parts > 0:
-            carry = lax.fori_loop(0, parts // 2, fuller, carry)
-        return lax.fori_loop(parts // 2, length, body, carry)[1]
+            return following
+
+        lax.fori_loop(0, length, body, prepare(stencil_at(1), direction))
+
+    finish_halo(pair_y, ext_y, cy, my, count_y)
+
+    def store_y(field, cell, value):
+        moved[field, cell] = value
+
+    sweep(ext_y, cy, 1, store_y)
 
     for step in range(1, count_x):
         arrived = tiles.at[lax.rem(mx - step + count_x, count_x)]
@@ -737,20 +742,12 @@
         splits[index, 0:16] = high
         splits[index, 16:32] = low
 
-    finish_halo(pair_y, ext_y, cy, my, count_y)
-
-    def store_y(field, cell, value):
-        moved[field, cell] = value
-
-    def partial_sum(index, total):
+    upper = jnp.zeros((32, wide), jnp.float32)
+    lower = jnp.zeros((16, wide), jnp.float32)
+    for index in range(chunks):
         both = splits[index]
-        return (
-            total[0] + product(both, table["window_hi"][index]),
-            total[1] + product(both[:16], table["window_lo"][index]),
-        )
-
-    zeros = jnp.zeros((32, wide), jnp.float32), jnp.zeros((16, wide), jnp.float32)
-    upper, lower = sweep(ext_y, cy, 1, store_y, partial_sum, zeros, chunks)
+        upper = upper + product(both, table["window_hi"][index])
+        lower = lower + product(both[:16], table["window_lo"][index])
     sums = (upper[:16] + upper[16:] + lower) * table["scale"][...]
 
 
@@ -786,10 +783,10 @@
     from_two = jnp.where(same_half, picked(table["take_two"][...], second_sum), 0.0)
     which_one = px * 2 + py
     first_sum = picked(table["take_one"][...], select(sums, which_one)) + times(
-        from_two, table["down_two_hi"][which_one], table["down_two_lo"][which_one]
+        from_two, *pair_of("down_two", which_one)
     )
     from_one = jnp.where(same_half, picked(table["take_zero"][...], first_sum), 0.0)
-    expansion = sums[0:8] + times(from_one, table["down_one_hi"][...], table["down_one_lo"][...])
+    expansion = sums[0:8] + times(from_one, *pair_of("down_one"))
     turned_hi, turned_lo = halves(expansion.T)
     to_z = table["to_z"][...].astype(jnp.bfloat16)
     on_z = product(turned_hi, to_z) + product(turned_lo, to_z)
@@ -798,7 +795,9 @@
         high, low = halves(on_z * table["weights"][which])
         field_hi = table["fields_hi"][first_row:last_row]
         piece = product(field_hi, high) + product(field_hi, low)
-        pieces.append(piece + product(table["fields_lo"][first_row:last_row], high))
+        if "fields_lo" in names:
+            piece = piece + product(table["fields_lo"][first_row:last_row], high)
+        pieces.append(piece)
     for k in range(3):
         parts = pieces[0][k * 96 : k * 96 + 96] if k < 2 else pieces[1]
         for row in range(cx):
@@ -836,7 +835,8 @@
     for name, array in (("flag_z", flag_z), ("cell_rows", cell_rows), ("along_z", along_z)):
         constants[name] = jnp.asarray(array, jnp.float32)
     for name, array in (("spread", spread), ("pick_up", pick_up), ("second", second)):
-        constants[name + "_hi"], constants[name + "_lo"] = split_pair(array)
+        for ending, part in split_pair(array):
+            constants[name + ending] = jnp.asarray(part)
     for name, array in (("one_rows", one_rows), ("two_rows", two_rows)):
         constants[name] = jnp.asarray(array, jnp.float32)
     joined = np.concatenate([middle, close]).reshape(-1, wide, wide)
@@ -844,7 +844,8 @@
         ("window", joined), ("down_two", down_two), ("down_one", down_one),
         ("fields", fields.reshape(-1, wide)),
     ):
-        constants[name + "_hi"], constants[name + "_lo"] = split_pair(array)
+        for ending, part in split_pair(array):
+            constants[name + ending] = jnp.asarray(part)
     for name, array in (
         ("scale", scale), ("take_one", take_one), ("take_two", take_two),
         ("take_zero", take_zero), ("to_z", to_z), ("weights", weights),

time: 41.3 us -> 38.5 us (0.932)
  local copies, waits for them, and re-layouts: 5.86 us -> 3.79 us
  Pallas kernels: 34.7 us -> 33.9 us
    convert_element_type x3 -> x0, local copies, waits for them, and re-layouts: 2.06 us -> none  [split_pair(): return (high, (table - high.astype(jnp.float32)).astype(jnp.bfloat16))]
    pallas_call x1, Pallas kernels: 34.7 us -> 33.9 us  [shards(): pl.pallas_call(functools.partial(section_kernel, (count_x, count_y, nf, c...]
where the time goes in v4:
time: 38.5 us; the launch traced here: 38.3 us
  Pallas kernels  33.9 us (88%)
  local copies, waits for them, and re-layouts  3.79 us (10%)
  between operations  0.65 us (2%)
    pallas_call x1, Pallas kernels, shards(): pl.pallas_call(functools.partial(section_kernel, (count_x, count_y, nf, c...  33.9 us
    unnamed x4, local copies, waits for them, and re-layouts  3.79 us

profile of v4, /device:TPU:0, one launch (start us, length us, event | category | flops | bytes accessed | tf_op | source)
XLA Modules:
  0.0 38.3 jit_solution(5150472724573403637)
XLA Ops:
  0.6 33.9 %shard_map.275 = (f32[15,16,16,128]{3,2,1,0:T(8,128)}, f32[3,16,16,128]{3,2,1,0:T(8,128)}) custom-call(f32[1,16,16,128]{3,2,1,0:T(8,128)} %bitcast.3, f32[3,16,16,128]{3,2,1,0:T(8,128)} %momentum.1, f32[1,16,16,128]{3,2,1,0:T(8,128)} %bitcast.4, f32[1,16,16,128]{3,2,1,0:T(8,128)} %bitcast.5, f32[9,16,16,128]{3,2,1,0:T(8,128)} %tracers.1, s32[2,2,16]{2,1,0:T(2,128)} %flags.1, ...), custom_call_target="tpu_custom_call" | custom-call | tf_op jit(solution)/shard_map/pallas_call | solution.py:868
  34.5 0.0 copy-start
  34.5 3.0 %copy.32 = f32[15,16,16,128]{3,2,1,0:T(8,128)} copy(f32[15,16,16,128]{3,2,1,0:T(8,128)} %get-tuple-element.4) | data formatting | bytes 3932160
  37.6 0.0 copy-done
  37.6 0.7 %copy.33 = f32[3,16,16,128]{3,2,1,0:T(8,128)} copy(f32[3,16,16,128]{3,2,1,0:T(8,128)S(1)} %copy-done) | data formatting | bytes 786432
Async XLA Ops:
  34.5 3.1 %copy-start = (f32[3,16,16,128]{3,2,1,0:T(8,128)S(1)}, f32[3,16,16,128]{3,2,1,0:T(8,128)}, u32[]{:S(2)}) copy-start(f32[3,16,16,128]{3,2,1,0:T(8,128)} %get-tuple-element.5) | copy-start | bytes 1179652

commit v5 on v4

--- a/solution.py
+++ b/solution.py
@@ -481,15 +481,19 @@
     pair_x = halo_pair(ext_x, cx, 0, at_x)
     pair_y = halo_pair(ext_y, cy, 2, at_y)
 
-    def turn(field, carry):
-        for row in range(cy):
-            ext_y[field, 3 + row] = ext_x[field, pl.ds(3, cx), row, :]
-        return carry
-
-    lax.fori_loop(0, nf, turn, 0)
+    def turn(rows):
+        def one(field, carry):
+            for row in rows:
+                ext_y[field, 3 + row] = ext_x[field, pl.ds(3, cx), row, :]
+            return carry
+
+        lax.fori_loop(0, nf, one, 0)
+
+    turn([*range(3), *range(cy - 3, cy)])
     pl.semaphore_wait(barrier, count_x + count_y - 2)
     start_halo(pair_y, my, count_y)
     start_halo(pair_x, mx, count_x)
+    turn(range(3, cy - 3))
 
     planes = 4
 
@@ -559,16 +563,16 @@
     row_index = lax.broadcasted_iota(jnp.int32, (8, slot), 0)
     tiles[mx, my] = jnp.where(row_index == 7, best, tile)
 
-    for step in range(1, count_y):
+    for step in range(1, count_x):
         remote(
             tiles.at[mx, my], tiles.at[mx, my],
-            first_send.at[step], first_recv.at[step], at_y(step),
+            first_send.at[step], first_recv.at[step], at_x(step),
         ).start()
-    side_y = (
-        remote(near.at[1, 1], near.at[1, 2], side_send.at[0], side_recv.at[0], at_y(-1)),
-        remote(near.at[1, 1], near.at[1, 0], side_send.at[1], side_recv.at[1], at_y(1)),
+    side_x = (
+        remote(near.at[1, 1], near.at[2, 1], side_send.at[0], side_recv.at[0], at_x(-1)),
+        remote(near.at[1, 1], near.at[0, 1], side_send.at[1], side_recv.at[1], at_x(1)),
     )
-    start_halo(side_y, my, count_y)
+    start_halo(side_x, mx, count_x)
 
     lane_z = lax.broadcasted_iota(jnp.int32, (cy, cz), 1)
 
@@ -616,13 +620,7 @@
         apply(prepared, stencil_z(row), 2, nf, emit)
         return following
 
-    half_way = lax.fori_loop(0, cx // 2, sweep_z, prepare(stencil_z(0), 2))
-
-    for step in range(1, count_y):
-        arrived = tiles.at[mx, lax.rem(my - step + count_y, count_y)]
-        copy = remote(arrived, arrived, first_send.at[step], first_recv.at[step], at_y(step))
-        copy.wait_send()
-        copy.wait_recv()
+    lax.fori_loop(0, cx, sweep_z, prepare(stencil_z(0), 2))
 
     def finish_side(pair, position, count, low, high):
         @pl.when(position > 0)
@@ -643,18 +641,22 @@
         def _():
             high[...] = jnp.zeros(high.shape, jnp.float32)
 
-    finish_side(side_y, my, count_y, near.at[1, 0], near.at[1, 2])
     for step in range(1, count_x):
+        arrived = tiles.at[lax.rem(mx - step + count_x, count_x), my]
+        copy = remote(arrived, arrived, first_send.at[step], first_recv.at[step], at_x(step))
+        copy.wait_send()
+        copy.wait_recv()
+    finish_side(side_x, mx, count_x, near.at[0, 1], near.at[2, 1])
+    for step in range(1, count_y):
         remote(
-            tiles.at[mx], tiles.at[mx], second_send.at[step], second_recv.at[step], at_x(step)
+            tiles.at[:, my], tiles.at[:, my], second_send.at[step], second_recv.at[step], at_y(step)
         ).start()
-    side_x = (
-        remote(near.at[1], near.at[2], side_send.at[2], side_recv.at[2], at_x(-1)),
-        remote(near.at[1], near.at[0], side_send.at[3], side_recv.at[3], at_x(1)),
+    side_y = (
+        remote(near.at[:, 1], near.at[:, 2], side_send.at[2], side_recv.at[2], at_y(-1)),
+        remote(near.at[:, 1], near.at[:, 0], side_send.at[3], side_recv.at[3], at_y(1)),
     )
-    start_halo(side_x, mx, count_x)
-
-    lax.fori_loop(cx // 2, cx, sweep_z, half_way)
+    start_halo(side_y, my, count_y)
+
 
     def sweep(buffer, length, direction, store):
         def stencil_at(face):
@@ -677,6 +679,13 @@
 
         lax.fori_loop(0, length, body, prepare(stencil_at(1), direction))
 
+    finish_halo(pair_x, ext_x, cx, mx, count_x)
+
+    def store_x(field, cell, value):
+        section[field, cell] = section[field, cell] + value
+
+    sweep(ext_x, cx, 0, store_x)
+
     finish_halo(pair_y, ext_y, cy, my, count_y)
 
     def store_y(field, cell, value):
@@ -684,12 +693,12 @@
 
     sweep(ext_y, cy, 1, store_y)
 
-    for step in range(1, count_x):
-        arrived = tiles.at[lax.rem(mx - step + count_x, count_x)]
-        copy = remote(arrived, arrived, second_send.at[step], second_recv.at[step], at_x(step))
+    for step in range(1, count_y):
+        arrived = tiles.at[:, lax.rem(my - step + count_y, count_y)]
+        copy = remote(arrived, arrived, second_send.at[step], second_recv.at[step], at_y(step))
         copy.wait_send()
         copy.wait_recv()
-    finish_side(side_x, mx, count_x, near.at[0], near.at[2])
+    finish_side(side_y, my, count_y, near.at[:, 0], near.at[:, 2])
 
     fastest = jnp.max(jnp.max(tiles[...], axis=(0, 1))[7:8, :])
     step_size = courant / (SUB * jnp.full((1, cz), fastest, jnp.float32))
@@ -809,18 +818,19 @@
                 + (height * height) * parts[base + 4 * SUB : base + 6 * SUB]
             )
 
-    finish_halo(pair_x, ext_x, cx, mx, count_x)
-
-    def store_x(field, cell, value):
-        total = (value + section[field, cell] + moved[field, :, cell, :]) * (-float(SUB))
-        if 1 <= field <= 3:
-            total = total + ext_x[0, 3 + cell] * accel[field - 1, cell]
-        if field == 4:
-            for k in range(3):
-                total = total + ext_x[1 + k, 3 + cell] * accel[k, cell]
-        section[field, cell] = ext_x[field, 3 + cell] + step_size * total
-
-    sweep(ext_x, cx, 0, store_x)
+    def finish(cell, carry):
+        own = [ext_x[field, 3 + cell] for field in range(4)]
+        pull = [accel[k, cell] for k in range(3)]
+        for field in range(nf):
+            total = (section[field, cell] + moved[field, :, cell, :]) * (-float(SUB))
+            if 1 <= field <= 3:
+                total = total + own[0] * pull[field - 1]
+            if field == 4:
+                total = total + own[1] * pull[0] + own[2] * pull[1] + own[3] * pull[2]
+            section[field, cell] = ext_x[field, 3 + cell] + step_size * total
+        return carry
+
+    lax.fori_loop(0, cx, finish, 0)
 
 
 def shards(density, momentum, energy, entropy, tracers, leaf_flags):
@@ -887,7 +897,7 @@
             pltpu.VMEM((128, cz), f32),
             pltpu.VMEM((joined.shape[0], 32, wide), jnp.bfloat16),
             dma((5,)), dma((len(names),)), dma((4,)), dma((4,)),
-            dma((count_y,)), dma((count_y,)), dma((count_x,)), dma((count_x,)),
+            dma((count_x,)), dma((count_x,)), dma((count_y,)), dma((count_y,)),
             dma((4,)), dma((4,)),
         ],
         compiler_params=pltpu.CompilerParams(

time: 38.5 us -> 35.7 us (0.927)
  Pallas kernels: 33.9 us -> 31.1 us
    pallas_call x1, Pallas kernels: 33.9 us -> 31.1 us  [shards(): pl.pallas_call(functools.partial(section_kernel, (count_x, count_y, nf, c...]
where the time goes in v5:
time: 35.7 us; the launch traced here: 35.5 us
  Pallas kernels  31.1 us (87%)
  local copies, waits for them, and re-layouts  3.79 us (11%)
  between operations  0.65 us (2%)
    pallas_call x1, Pallas kernels, shards(): pl.pallas_call(functools.partial(section_kernel, (count_x, count_y, nf, c...  31.1 us
    unnamed x4, local copies, waits for them, and re-layouts  3.79 us

profile of v5, /device:TPU:0, one launch (start us, length us, event | category | flops | bytes accessed | tf_op | source)
XLA Modules:
  0.0 35.5 jit_solution(7209742979164359509)
XLA Ops:
  0.6 31.1 %shard_map.275 = (f32[15,16,16,128]{3,2,1,0:T(8,128)}, f32[3,16,16,128]{3,2,1,0:T(8,128)}) custom-call(f32[1,16,16,128]{3,2,1,0:T(8,128)} %bitcast.3, f32[3,16,16,128]{3,2,1,0:T(8,128)} %momentum.1, f32[1,16,16,128]{3,2,1,0:T(8,128)} %bitcast.4, f32[1,16,16,128]{3,2,1,0:T(8,128)} %bitcast.5, f32[9,16,16,128]{3,2,1,0:T(8,128)} %tracers.1, s32[2,2,16]{2,1,0:T(2,128)} %flags.1, ...), custom_call_target="tpu_custom_call" | custom-call | tf_op jit(solution)/shard_map/pallas_call | solution.py:878
  31.7 0.0 copy-start
  31.7 3.0 %copy.32 = f32[15,16,16,128]{3,2,1,0:T(8,128)} copy(f32[15,16,16,128]{3,2,1,0:T(8,128)} %get-tuple-element.4) | data formatting | bytes 3932160
  34.8 0.0 copy-done
  34.8 0.7 %copy.33 = f32[3,16,16,128]{3,2,1,0:T(8,128)} copy(f32[3,16,16,128]{3,2,1,0:T(8,128)S(1)} %copy-done) | data formatting | bytes 786432
Async XLA Ops:
  31.7 3.1 %copy-start = (f32[3,16,16,128]{3,2,1,0:T(8,128)S(1)}, f32[3,16,16,128]{3,2,1,0:T(8,128)}, u32[]{:S(2)}) copy-start(f32[3,16,16,128]{3,2,1,0:T(8,128)} %get-tuple-element.5) | copy-start | bytes 1179652

commit v6 on v5

--- a/solution.py
+++ b/solution.py
@@ -390,10 +390,11 @@
     sizes, top, names, density, momentum, energy, entropy, tracers, flags, *rest
 ):
     held_tables = dict(zip(names, rest[: len(names)]))
-    section, accel = rest[len(names) : len(names) + 2]
+    section_out, accel_out = rest[len(names) : len(names) + 2]
     table = dict(zip(names, rest[len(names) + 2 : 2 * len(names) + 2]))
     (
         ext_x, ext_y, moved, previous, packed, packed_flux, tiles, near, window, rows_p, splits,
+        section, accel, out_sem,
         load_sem, table_sem, halo_send, halo_recv, first_send, first_recv,
         second_send, second_recv, side_send, side_recv,
     ) = rest[2 * len(names) + 2 :]
@@ -830,7 +831,32 @@
             section[field, cell] = ext_x[field, 3 + cell] + step_size * total
         return carry
 
-    lax.fori_loop(0, cx, finish, 0)
+    leaving = [pltpu.make_async_copy(accel, accel_out, out_sem.at[4])]
+    leaving[0].start()
+    for quarter in range(4):
+        begin = quarter * cx // 4
+        lax.fori_loop(begin, begin + cx // 4, finish, 0)
+        planes_out = pl.ds(begin, cx // 4)
+        leaving.append(
+            pltpu.make_async_copy(
+                section.at[:, planes_out], section_out.at[:, planes_out], out_sem.at[quarter]
+            )
+        )
+        leaving[-1].start()
+    for copy in leaving:
+        copy.wait()
+
+
+def hand_over_kernel(section, accel, section_out, accel_out, sem):
+    copies = [
+        pltpu.make_async_copy(source.at[i], target.at[i], sem.at[base + i])
+        for base, source, target in ((0, section, section_out), (section.shape[0], accel, accel_out))
+        for i in range(source.shape[0])
+    ]
+    for copy in copies:
+        copy.start()
+    for copy in copies:
+        copy.wait()
 
 
 def shards(density, momentum, energy, entropy, tracers, leaf_flags):
@@ -875,14 +901,15 @@
     local = pl.BlockSpec(memory_space=pltpu.VMEM)
     dma = pltpu.SemaphoreType.DMA
     f32 = jnp.float32
-    return pl.pallas_call(
+    out_shape = (
+        jax.ShapeDtypeStruct((nf, cx, cy, cz), f32),
+        jax.ShapeDtypeStruct((3, cx, cy, cz), f32),
+    )
+    results = pl.pallas_call(
         functools.partial(section_kernel, (count_x, count_y, nf, cx, cy, cz), top, names),
-        out_shape=(
-            jax.ShapeDtypeStruct((nf, cx, cy, cz), f32),
-            jax.ShapeDtypeStruct((3, cx, cy, cz), f32),
-        ),
+        out_shape=out_shape,
         in_specs=[anywhere] * 5 + [local] + [anywhere] * len(names),
-        out_specs=(local, local),
+        out_specs=(anywhere, anywhere),
         scratch_shapes=shapes
         + [
             pltpu.VMEM((nf, cx + 6, cy, cz), f32),
@@ -896,6 +923,9 @@
             pltpu.VMEM((16, 36 * slot), f32),
             pltpu.VMEM((128, cz), f32),
             pltpu.VMEM((joined.shape[0], 32, wide), jnp.bfloat16),
+            pltpu.VMEM((nf, cx, cy, cz), f32),
+            pltpu.VMEM((3, cx, cy, cz), f32),
+            dma((5,)),
             dma((5,)), dma((len(names),)), dma((4,)), dma((4,)),
             dma((count_x,)), dma((count_x,)), dma((count_y,)), dma((count_y,)),
             dma((4,)), dma((4,)),
@@ -904,6 +934,13 @@
             collective_id=0, has_side_effects=True, vmem_limit_bytes=56 * 1024 * 1024
         ),
     )(density[None], momentum, energy[None], entropy[None], tracers, leaf_flags, *constants.values())
+    return pl.pallas_call(
+        hand_over_kernel,
+        out_shape=out_shape,
+        in_specs=[anywhere] * 2,
+        out_specs=(anywhere, anywhere),
+        scratch_shapes=[dma((nf + 3,))],
+    )(*results)
 
 
 def solution(mesh):

time: 35.7 us -> 104 us (2.91)
  Pallas kernels: 31.1 us -> 103 us
  local copies, waits for them, and re-layouts: 3.79 us -> 0 us
    pallas_call x0 -> x1, Pallas kernels: none -> 72.7 us  [shards(): pl.pallas_call(hand_over_kernel, out_shape=out_shape, in_specs=[anywhere]...]
    unnamed x4 -> x0, local copies, waits for them, and re-layouts: 3.79 us -> none
where the time goes in v6:
time: 104 us
  Pallas kernels  103 us (99%)
    pallas_call x1, Pallas kernels, shards(): pl.pallas_call(hand_over_kernel, out_shape=out_shape, in_specs=[anywhere]...  72.7 us
    pallas_call x1, Pallas kernels, shards(): pl.pallas_call(functools.partial(section_kernel, (count_x, count_y, nf, c...  30.6 us

profile of v6, /device:TPU:0, one launch (start us, length us, event | category | flops | bytes accessed | tf_op | source)
XLA Modules:
  0.0 104.0 jit_solution(16158337812426935429)
XLA Ops:
  0.6 30.6 %shard_map.275 = (f32[15,16,16,128]{3,2,1,0:T(8,128)}, f32[3,16,16,128]{3,2,1,0:T(8,128)}) custom-call(f32[1,16,16,128]{3,2,1,0:T(8,128)} %bitcast.3, f32[3,16,16,128]{3,2,1,0:T(8,128)} %momentum.1, f32[1,16,16,128]{3,2,1,0:T(8,128)} %bitcast.4, f32[1,16,16,128]{3,2,1,0:T(8,128)} %bitcast.5, f32[9,16,16,128]{3,2,1,0:T(8,128)} %tracers.1, s32[2,2,16]{2,1,0:T(2,128)} %flags.1, ...), custom_call_target="tpu_custom_call" | custom-call | tf_op jit(solution)/shard_map/pallas_call | solution.py:908
  31.3 72.7 %shard_map.276 = (f32[15,16,16,128]{3,2,1,0:T(8,128)}, f32[3,16,16,128]{3,2,1,0:T(8,128)}) custom-call(f32[15,16,16,128]{3,2,1,0:T(8,128)} %get-tuple-element.4.section, f32[3,16,16,128]{3,2,1,0:T(8,128)} %get-tuple-element.5.accel), custom_call_target="tpu_custom_call" | custom-call | tf_op jit(solution)/shard_map/pallas_call | solution.py:937

commit v7 on v6

--- a/solution.py
+++ b/solution.py
@@ -847,15 +847,24 @@
         copy.wait()
 
 
-def hand_over_kernel(section, accel, section_out, accel_out, sem):
-    copies = [
-        pltpu.make_async_copy(source.at[i], target.at[i], sem.at[base + i])
-        for base, source, target in ((0, section, section_out), (section.shape[0], accel, accel_out))
-        for i in range(source.shape[0])
+def hand_over_kernel(section, accel, section_out, accel_out, staged, in_sem, out_sem):
+    count = section.shape[0]
+    pieces = [(section.at[i], section_out.at[i]) for i in range(count)]
+    pieces += [(accel.at[i], accel_out.at[i]) for i in range(accel.shape[0])]
+    arriving = [
+        pltpu.make_async_copy(source, staged.at[i], in_sem.at[i])
+        for i, (source, _) in enumerate(pieces)
     ]
-    for copy in copies:
+    leaving = [
+        pltpu.make_async_copy(staged.at[i], target, out_sem.at[i])
+        for i, (_, target) in enumerate(pieces)
+    ]
+    for copy in arriving:
         copy.start()
-    for copy in copies:
+    for before, after in zip(arriving, leaving):
+        before.wait()
+        after.start()
+    for copy in leaving:
         copy.wait()
 
 
@@ -939,7 +948,7 @@
         out_shape=out_shape,
         in_specs=[anywhere] * 2,
         out_specs=(anywhere, anywhere),
-        scratch_shapes=[dma((nf + 3,))],
+        scratch_shapes=[pltpu.VMEM((nf + 3, cx, cy, cz), f32), dma((nf + 3,)), dma((nf + 3,))],
     )(*results)
 
 

time: 104 us -> 34.1 us (0.33)
  Pallas kernels: 103 us -> 33.3 us
    pallas_call x1, Pallas kernels: 72.7 us -> 2.69 us  [shards(): pl.pallas_call(hand_over_kernel, out_shape=out_shape, in_specs=[anywhere]...]
where the time goes in v7:
time: 34.1 us; the launch traced here: 34 us
  Pallas kernels  33.3 us (98%)
  between operations  0.64 us (2%)
    pallas_call x1, Pallas kernels, shards(): pl.pallas_call(functools.partial(section_kernel, (count_x, count_y, nf, c...  30.6 us
    pallas_call x1, Pallas kernels, shards(): pl.pallas_call(hand_over_kernel, out_shape=out_shape, in_specs=[anywhere]...  2.69 us

profile of v7, /device:TPU:0, one launch (start us, length us, event | category | flops | bytes accessed | tf_op | source)
XLA Modules:
  0.0 34.0 jit_solution(14914910848172815740)
XLA Ops:
  0.6 30.6 %shard_map.275 = (f32[15,16,16,128]{3,2,1,0:T(8,128)}, f32[3,16,16,128]{3,2,1,0:T(8,128)}) custom-call(f32[1,16,16,128]{3,2,1,0:T(8,128)} %bitcast.3, f32[3,16,16,128]{3,2,1,0:T(8,128)} %momentum.1, f32[1,16,16,128]{3,2,1,0:T(8,128)} %bitcast.4, f32[1,16,16,128]{3,2,1,0:T(8,128)} %bitcast.5, f32[9,16,16,128]{3,2,1,0:T(8,128)} %tracers.1, s32[2,2,16]{2,1,0:T(2,128)} %flags.1, ...), custom_call_target="tpu_custom_call" | custom-call | tf_op jit(solution)/shard_map/pallas_call | solution.py:917
  31.3 2.7 %shard_map.276 = (f32[15,16,16,128]{3,2,1,0:T(8,128)}, f32[3,16,16,128]{3,2,1,0:T(8,128)}) custom-call(f32[15,16,16,128]{3,2,1,0:T(8,128)} %get-tuple-element.4.section, f32[3,16,16,128]{3,2,1,0:T(8,128)} %get-tuple-element.5.accel), custom_call_target="tpu_custom_call" | custom-call | tf_op jit(solution)/shard_map/pallas_call | solution.py:946

commit v8 on v7

--- a/solution.py
+++ b/solution.py
@@ -621,7 +621,7 @@
         apply(prepared, stencil_z(row), 2, nf, emit)
         return following
 
-    lax.fori_loop(0, cx, sweep_z, prepare(stencil_z(0), 2))
+    lax.fori_loop(0, cx, sweep_z, prepare(stencil_z(0), 2), unroll=2)
 
     def finish_side(pair, position, count, low, high):
         @pl.when(position > 0)
@@ -678,7 +678,7 @@
             apply(prepared, stencil_at(cell + 1), direction, nf, emit)
             return following
 
-        lax.fori_loop(0, length, body, prepare(stencil_at(1), direction))
+        lax.fori_loop(0, length, body, prepare(stencil_at(1), direction), unroll=2)
 
     finish_halo(pair_x, ext_x, cx, mx, count_x)
 

time: 34.1 us -> 53.8 us (1.58)
  Pallas kernels: 33.3 us -> 53 us
    pallas_call x1, Pallas kernels: 30.6 us -> 50.3 us  [shards(): pl.pallas_call(functools.partial(section_kernel, (count_x, count_y, nf, c...]
where the time goes in v8:
time: 53.8 us; the launch traced here: 53.6 us
  Pallas kernels  53 us (99%)
  between operations  0.64 us (1%)
    pallas_call x1, Pallas kernels, shards(): pl.pallas_call(functools.partial(section_kernel, (count_x, count_y, nf, c...  50.3 us
    pallas_call x1, Pallas kernels, shards(): pl.pallas_call(hand_over_kernel, out_shape=out_shape, in_specs=[anywhere]...  2.69 us

profile of v8, /device:TPU:0, one launch (start us, length us, event | category | flops | bytes accessed | tf_op | source)
XLA Modules:
  0.0 53.6 jit_solution(7256907383747277236)
XLA Ops:
  0.6 50.3 %shard_map.275 = (f32[15,16,16,128]{3,2,1,0:T(8,128)}, f32[3,16,16,128]{3,2,1,0:T(8,128)}) custom-call(f32[1,16,16,128]{3,2,1,0:T(8,128)} %bitcast.3, f32[3,16,16,128]{3,2,1,0:T(8,128)} %momentum.1, f32[1,16,16,128]{3,2,1,0:T(8,128)} %bitcast.4, f32[1,16,16,128]{3,2,1,0:T(8,128)} %bitcast.5, f32[9,16,16,128]{3,2,1,0:T(8,128)} %tracers.1, s32[2,2,16]{2,1,0:T(2,128)} %flags.1, ...), custom_call_target="tpu_custom_call" | custom-call | tf_op jit(solution)/shard_map/pallas_call | solution.py:917
  50.9 2.7 %shard_map.276 = (f32[15,16,16,128]{3,2,1,0:T(8,128)}, f32[3,16,16,128]{3,2,1,0:T(8,128)}) custom-call(f32[15,16,16,128]{3,2,1,0:T(8,128)} %get-tuple-element.4.section, f32[3,16,16,128]{3,2,1,0:T(8,128)} %get-tuple-element.5.accel), custom_call_target="tpu_custom_call" | custom-call | tf_op jit(solution)/shard_map/pallas_call | solution.py:946
